TPU v7x, 32 devices: a whole 2x2x4 slice. The times are simulated.
32 devices in a mesh: groups: 2 (over x), paths: 2 (over core), feats: 8 (over z, y).
Axes of the slice: x: 2, y: 2, z: 4, core: 2. Of those that a mesh axis runs over, the one named last changes fastest.
Arguments:
- factors: int32 [4096, 128], P(('groups', 'paths')), parts along dimension 0, may hold values from -8 to 8
- frequency: int32 [128, 65536], P(None, 'feats'), may hold values from -48 to 48
- phases: int32 [65536], P('feats'), may hold values from 0 to 1023
- amplitude: float32 [65536], P('feats'), as said below
- targets: float32 [32, 4096], P(None, ('groups', 'paths')), parts along dimension 1, may hold values from -6 to 6
- coeffs_init: float32 [32, 131072], P(None, ('groups', 'feats')), parts along dimension 1, may hold values from -6 to 6
Outputs:
- coeffs: float32 [32, 131072], P(None, ('groups', 'feats')), parts along dimension 1
- predicted: float32 [32, 4096], P(None, ('groups', 'paths')), parts along dimension 1
There are 2 independent parts, one for each index of `groups`. A program takes and returns all parts, laid end to end along the dimension named above; an argument that names none is the same for every part. Nothing has to cross between parts.
Inputs may be any that keep to these rules, and one draw needn't show every extreme that they name: `amplitude`: positive feature weights.
All inputs are finite; a program needn't handle non-finite values.
Results may differ from a plain program's by a relative error of at most 0.00026.
Values sent between devices are 32-bit elements; how exact they have to be, the bound alone decides.
No kernel may reach another device: no remote copies, remote signals or barrier semaphores. Data moves between devices by JAX's collectives and lax.ppermute only.
A program may use at most 128 MiB of HBM per device.

v0:
```python
import math

import jax
import jax.numpy as jnp
from jax import lax
from jax.sharding import PartitionSpec as P

F = 65536
V = 32
ITERS = 3


huber_cap = 1.0
step_rate = 0.2
momentum = 0.9
epsilon = 1e-06


def build(factor_vals, freq_block, phase_block, amp_block):
    summed = jnp.dot(
        factor_vals, freq_block, precision=lax.Precision.HIGHEST, preferred_element_type=jnp.float32
    )
    return amp_block * jnp.cos(summed * 0.0025 + phase_block * (2.0 * math.pi / 1024.0))


def image_of(coeffs, block):
    return lax.dot_general(
        coeffs,
        block,
        (((1,), (1,)), ((), ())),
        precision=lax.Precision.HIGHEST,
        preferred_element_type=jnp.float32,
    )


def shards(factors, frequency, phases, amplitude, targets, coeffs_init):
    factor_vals = factors.astype(jnp.float32)
    freq_vals = frequency.astype(jnp.float32)
    phase_vals = phases.astype(jnp.float32)
    stored = build(factor_vals, freq_vals, phase_vals, amplitude)

    def features_now():
        return stored

    coeffs = coeffs_init
    velocity = jnp.zeros_like(coeffs_init)
    tracked = jnp.zeros_like(targets)
    predicted = lax.psum(image_of(coeffs, features_now()), "feats")
    for turn in range(ITERS):
        block = features_now()
        clipped = jnp.clip(predicted - targets, -huber_cap, huber_cap)
        local_grad = jnp.dot(
            clipped, block, precision=lax.Precision.HIGHEST, preferred_element_type=jnp.float32
        )
        gradient = lax.psum(local_grad, "paths")
        pushed, squares = lax.psum(
            (image_of(gradient, block), jnp.sum(gradient * gradient)), "feats"
        )
        scale = jnp.sqrt(squares / (V * F) + epsilon)
        velocity = momentum * velocity + gradient / scale
        coeffs = coeffs - step_rate * velocity
        tracked = momentum * tracked + pushed / scale
        predicted = predicted - step_rate * tracked
    return (coeffs, predicted)


def solution(mesh):
    return jax.shard_map(
        shards,
        mesh=mesh,
        in_specs=(
            P(("groups", "paths"), None),
            P(None, "feats"),
            P("feats"),
            P("feats"),
            P(None, ("groups", "paths")),
            P(None, ("groups", "feats")),
        ),
        out_specs=(P(None, ("groups", "feats")), P(None, ("groups", "paths"))),
        check_vma=False,
    )
```

profile of v0, /device:TPU:0, one launch (start us, length us, event | category | flops | bytes accessed | tf_op | source)
XLA Modules:
  0.0 750.3 jit_solution(18103428148732155704)
XLA Ops:
  7.2 0.0 all-reduce.8.cloned.1.call-start
  7.2 0.8 convert_multiply_fusion
  8.1 139.3 %cosine_multiply_fusion = f32[1024,8192]{1,0:T(8,128)} fusion(f32[8192]{0:T(1024)S(1)} %convert_multiply_fusion, f32[8192]{0:T(1024)} %param.9, s32[128,8192]{1,0:T(8,128)} %param.7, s32[1024,128]{1,0:T(8,128)} %param.6), kind=kOutput, calls=%fused_computation | convolution fusion | flops 12911247360 | bytes 38338560 | tf_op jit(solution)/shard_map/dot_general | solution.py:20
  147.4 34.8 %convolution_bitcast_fusion = f32[32,1024]{1,0:T(8,128)} fusion(f32[1024,8192]{1,0:T(8,128)} %cosine_multiply_fusion, f32[32,8192]{1,0:T(8,128)S(1)} %copy-done.3), kind=kOutput, calls=%fused_computation.2 | convolution fusion | flops 3221225472 | bytes 34734080 | tf_op jit(solution)/shard_map/dot_general | solution.py:27
  182.2 0.2 all-reduce.10.cloned.1.call-start
  182.4 72.3 %all-reduce.8.cloned.1.call-done = f32[32,1024]{1,0:T(8,128)} async-done(((f32[32,1024]{1,0:T(8,128)}), f32[32,1024]{1,0:T(8,128)}) %all-reduce.8.cloned.1.call-update) | async-done | bytes 131088 | tf_op jit(solution)/shard_map/psum | solution.py:48
  254.7 30.2 %fusion.8 = f32[32,8192]{1,0:T(8,128)} fusion(f32[1024,8192]{1,0:T(8,128)} %cosine_multiply_fusion, f32[32,1024]{1,0:T(8,128)} %all-reduce.8.cloned.1.call-done, f32[32,1024]{1,0:T(8,128)S(1)} %copy-done.4), kind=kOutput, calls=%fused_computation.18 | convolution fusion | flops 3221291008 | bytes 34865152 | tf_op jit(solution)/shard_map/dot_general | solution.py:52
  285.0 0.4 all-reduce.12.cloned.1.call-start
  285.4 18.6 %all-reduce.10.cloned.1.call-done = f32[32,8192]{1,0:T(8,128)} async-done(((f32[32,8192]{1,0:T(8,128)}), f32[32,8192]{1,0:T(8,128)}) %all-reduce.10.cloned.1.call-update) | async-done | bytes 1048592 | tf_op jit(solution)/shard_map/psum | solution.py:55
  304.0 36.7 %fusion.25 = f32[32,1024]{1,0:T(8,128)} fusion(f32[32,8192]{1,0:T(8,128)} %all-reduce.10.cloned.1.call-done, f32[1024,8192]{1,0:T(8,128)} %cosine_multiply_fusion), kind=kOutput, calls=%fused_computation.37 | convolution fusion | flops 3221225472 | bytes 34734080 | tf_op jit(solution)/shard_map/dot_general | solution.py:27
  340.7 0.0 all-reduce.14.cloned.1.call-start
  340.8 0.9 multiply_reduce_fusion.2
  341.7 22.4 %psum.72 = f32[]{:T(128)} all-reduce(f32[]{:T(128)} %multiply_reduce_fusion.2), channel_id=1, replica_groups=mesh['groups'=2,'paths'=2,'feats'=8] {'feats'}, use_global_device_ids=true, to_apply=%region_3.4 | all-reduce | flops 1 | bytes 8 | tf_op jit(solution)/shard_map/psum | solution.py:56
  364.8 47.0 %all-reduce.12.cloned.1.call-done = f32[32,1024]{1,0:T(8,128)} async-done(((f32[32,1024]{1,0:T(8,128)}), f32[32,1024]{1,0:T(8,128)}) %all-reduce.12.cloned.1.call-update) | async-done | bytes 131088 | tf_op jit(solution)/shard_map/psum | solution.py:56
  411.8 0.9 multiply_subtract_fusion.3
  412.7 23.8 %fusion.5 = f32[32,8192]{1,0:T(8,128)} fusion(f32[1024,8192]{1,0:T(8,128)} %cosine_multiply_fusion, f32[32,1024]{1,0:T(8,128)S(1)} %multiply_subtract_fusion.3, f32[32,1024]{1,0:T(8,128)S(1)} %copy-done.4), kind=kOutput, calls=%fused_computation.14 | convolution fusion | flops 3221291008 | bytes 34865152 | tf_op jit(solution)/shard_map/dot_general | solution.py:52
  436.6 0.0 all-reduce.16.cloned.1.call-start
  436.6 19.0 %all-reduce.14.cloned.1.call-done = f32[32,8192]{1,0:T(8,128)} async-done(((f32[32,8192]{1,0:T(8,128)}), f32[32,8192]{1,0:T(8,128)}) %all-reduce.14.cloned.1.call-update) | async-done | bytes 1048592 | tf_op jit(solution)/shard_map/psum | solution.py:55
  455.6 36.7 %fusion.26 = f32[32,1024]{1,0:T(8,128)} fusion(f32[32,8192]{1,0:T(8,128)} %all-reduce.14.cloned.1.call-done, f32[1024,8192]{1,0:T(8,128)} %cosine_multiply_fusion), kind=kOutput, calls=%fused_computation.38 | convolution fusion | flops 3221225472 | bytes 34734080 | tf_op jit(solution)/shard_map/dot_general | solution.py:27
  492.4 0.0 all-reduce.18.cloned.1.call-start
  492.4 0.9 multiply_reduce_fusion.1
  493.3 22.7 %psum.75 = f32[]{:T(128)} all-reduce(f32[]{:T(128)} %multiply_reduce_fusion.1), channel_id=1, replica_groups=mesh['groups'=2,'paths'=2,'feats'=8] {'feats'}, use_global_device_ids=true, to_apply=%region_7.8 | all-reduce | flops 1 | bytes 8 | tf_op jit(solution)/shard_map/psum | solution.py:56
  516.7 46.6 %all-reduce.16.cloned.1.call-done = f32[32,1024]{1,0:T(8,128)} async-done(((f32[32,1024]{1,0:T(8,128)}), f32[32,1024]{1,0:T(8,128)}) %all-reduce.16.cloned.1.call-update) | async-done | bytes 131088 | tf_op jit(solution)/shard_map/psum | solution.py:56
  563.3 30.3 %fusion.2 = f32[32,8192]{1,0:T(8,128)} fusion(f32[1024,8192]{1,0:T(8,128)} %cosine_multiply_fusion, f32[32,1024]{1,0:T(8,128)S(1)} %copy-done.4, f32[32,1024]{1,0:T(8,128)S(1)} %multiply_subtract_fusion.3, f32[32,1024]{1,0:T(8,128)} %all-reduce.16.cloned.1.call-done, f32[]{:T(128)S(6)} %sqrt.10, f32[32,1024]{1,0:T(8,128)S(1)} %copy-done.5, f32[]{:T(128)S(6)} %sqrt.9), kind=kOutput, calls=%fused_computation.9 | convolution fusion | flops 3221487616 | bytes 35127304 | tf_op jit(solution)/shard_map/dot_general | solution.py:52
  593.6 0.0 all-reduce.20.cloned.1.call-start
  593.6 19.0 %all-reduce.18.cloned.1.call-done = f32[32,8192]{1,0:T(8,128)} async-done(((f32[32,8192]{1,0:T(8,128)}), f32[32,8192]{1,0:T(8,128)}) %all-reduce.18.cloned.1.call-update) | async-done | bytes 1048592 | tf_op jit(solution)/shard_map/psum | solution.py:55
  612.6 2.2 multiply_reduce_fusion
  614.8 22.4 %psum.78 = f32[]{:T(128)} all-reduce(f32[]{:T(128)} %multiply_reduce_fusion), channel_id=1, replica_groups=mesh['groups'=2,'paths'=2,'feats'=8] {'feats'}, use_global_device_ids=true, to_apply=%region_11.12 | all-reduce | flops 1 | bytes 8 | tf_op jit(solution)/shard_map/psum | solution.py:56
  637.9 36.7 %fusion.27 = f32[32,1024]{1,0:T(8,128)} fusion(f32[32,8192]{1,0:T(8,128)} %all-reduce.18.cloned.1.call-done, f32[1024,8192]{1,0:T(8,128)} %cosine_multiply_fusion), kind=kOutput, calls=%fused_computation.39 | convolution fusion | flops 3221225472 | bytes 34734080 | tf_op jit(solution)/shard_map/dot_general | solution.py:27
  674.6 2.6 multiply_subtract_fusion
  677.3 64.4 %all-reduce.20.cloned.1.call-done = f32[32,1024]{1,0:T(8,128)} async-done(((f32[32,1024]{1,0:T(8,128)}), f32[32,1024]{1,0:T(8,128)}) %all-reduce.20.cloned.1.call-update) | async-done | bytes 131088 | tf_op jit(solution)/shard_map/psum | solution.py:56
  741.6 1.6 multiply_subtract_fusion.1
  (23 shorter events, 0.1 us)
Async XLA Ops:
  7.2 140.2 %copy-start.3 = (f32[32,8192]{1,0:T(8,128)S(1)}, f32[32,8192]{1,0:T(8,128)}, u32[]{:S(2)}) copy-start(f32[32,8192]{1,0:T(8,128)} %param.11) | copy-start | bytes 3145732
  7.2 247.5 %all-reduce.8.cloned.1.call-start = ((), (), s32[]{:S(2)}) async-start(), calls=%async_computation | async-start | bytes 262144 | tf_op jit(solution)/shard_map/psum | solution.py:48
  8.1 246.6 %copy-start.4 = (f32[32,1024]{1,0:T(8,128)S(1)}, f32[32,1024]{1,0:T(8,128)}, u32[]{:S(2)}) copy-start(f32[32,1024]{1,0:T(8,128)} %param.10) | copy-start | bytes 393220
  182.2 121.8 %all-reduce.10.cloned.1.call-start = ((), (), s32[]{:S(2)}) async-start(), calls=%async_computation.1 | async-start | bytes 2097152 | tf_op jit(solution)/shard_map/psum | solution.py:55
  254.7 157.1 %copy-start.6 = (f32[32,1024]{1,0:T(8,128)S(1)}, f32[32,1024]{1,0:T(8,128)}, u32[]{:S(2)}) copy-start(f32[32,1024]{1,0:T(8,128)} %all-reduce.8.cloned.1.call-done) | copy-start | bytes 393220
  285.0 126.8 %all-reduce.12.cloned.1.call-start = ((), (), s32[]{:S(2)}) async-start(), calls=%async_computation.2 | async-start | bytes 262144 | tf_op jit(solution)/shard_map/psum | solution.py:56
  304.0 36.8 %copy-start = (f32[32,8192]{1,0:T(8,128)S(1)}, f32[32,8192]{1,0:T(8,128)}, u32[]{:S(2)}) copy-start(f32[32,8192]{1,0:T(8,128)} %all-reduce.10.cloned.1.call-done) | copy-start | bytes 3145732
  340.7 114.9 %all-reduce.14.cloned.1.call-start = ((), (), s32[]{:S(2)}) async-start(), calls=%async_computation.3 | async-start | bytes 2097152 | tf_op jit(solution)/shard_map/psum | solution.py:55
  412.7 150.6 %copy-start.5 = (f32[32,1024]{1,0:T(8,128)S(1)}, f32[32,1024]{1,0:T(8,128)}, u32[]{:S(2)}) copy-start(f32[32,1024]{1,0:T(8,128)} %all-reduce.12.cloned.1.call-done) | copy-start | bytes 393220
  436.6 126.7 %all-reduce.16.cloned.1.call-start = ((), (), s32[]{:S(2)}) async-start(), calls=%async_computation.4 | async-start | bytes 262144 | tf_op jit(solution)/shard_map/psum | solution.py:56
  455.6 36.8 %copy-start.1 = (f32[32,8192]{1,0:T(8,128)S(1)}, f32[32,8192]{1,0:T(8,128)}, u32[]{:S(2)}) copy-start(f32[32,8192]{1,0:T(8,128)} %all-reduce.14.cloned.1.call-done) | copy-start | bytes 3145732
  492.4 120.3 %all-reduce.18.cloned.1.call-start = ((), (), s32[]{:S(2)}) async-start(), calls=%async_computation.5 | async-start | bytes 2097152 | tf_op jit(solution)/shard_map/psum | solution.py:55
  563.3 178.3 %copy-start.7 = (f32[32,1024]{1,0:T(8,128)S(1)}, f32[32,1024]{1,0:T(8,128)}, u32[]{:S(2)}) copy-start(f32[32,1024]{1,0:T(8,128)} %all-reduce.16.cloned.1.call-done) | copy-start | bytes 393220
  593.6 148.0 %all-reduce.20.cloned.1.call-start = ((), (), s32[]{:S(2)}) async-start(), calls=%async_computation.6 | async-start | bytes 262144 | tf_op jit(solution)/shard_map/psum | solution.py:56
  612.6 62.0 %copy-start.2 = (f32[32,8192]{1,0:T(8,128)S(1)}, f32[32,8192]{1,0:T(8,128)}, u32[]{:S(2)}) copy-start(f32[32,8192]{1,0:T(8,128)} %all-reduce.18.cloned.1.call-done) | copy-start | bytes 3145732
Sparse Core Ops, SparseCore 0:
  182.3 72.3 all-reduce.7
  285.1 18.8 all-reduce.9
  340.9 70.8 all-reduce.11
  436.7 18.8 all-reduce.13
  492.5 70.7 all-reduce.15
  593.7 18.8 all-reduce.17
  674.7 66.8 all-reduce.19
where the time goes:
time: 758 us; the launch traced here: 750 us
  matrix products  369 us (49%)
  waiting for transfers between devices  287 us (38%)
  blocking collectives  67.5 us (9%)
  between operations  16.5 us (2%)
  other arithmetic  9.95 us (1%)
    psum x3, waiting for transfers between devices, shards(): lax.psum((image_of(gradient, block), jnp.sum(gradient * gradient)), 'feats')  158 us
    dot_general x4, matrix products, image_of(): lax.dot_general(coeffs, block, (((1,), (1,)), ((), ())), precision=lax.Pr...  145 us
    dot_general x1, matrix products, build(): jnp.dot(factor_vals, freq_block, precision=lax.Precision.HIGHEST, preferr...  139 us
    dot_general x3, matrix products, shards(): jnp.dot(clipped, block, precision=lax.Precision.HIGHEST, preferred_elemen...  84.4 us
    psum x1, waiting for transfers between devices, shards(): predicted = lax.psum(image_of(coeffs, features_now()), 'feats')  72.3 us
    psum x3, blocking collectives, shards(): lax.psum((image_of(gradient, block), jnp.sum(gradient * gradient)), 'feats')  67.5 us
    psum x3, waiting for transfers between devices, shards(): gradient = lax.psum(local_grad, 'paths')  56.5 us
  transfers between devices with their start and end apart: 7, of which 7 were waited for; matrix products, arithmetic and copies ran while one was open for 1% of the time, Pallas kernels for 0%

commit v1 on v0

v1 whole, which is shorter than its diff:
```python
import functools
import math

import jax
import jax.numpy as jnp
from jax import lax
from jax.experimental import pallas as pl
from jax.experimental.pallas import tpu as pltpu
from jax.sharding import PartitionSpec as P

ITERS = 3

huber_cap = 1.0
step_rate = 0.2
momentum = 0.9
epsilon = 1e-06

f32 = jnp.float32
bf16 = jnp.bfloat16

SIN = None


def fit_sine(terms):
    import numpy as np

    nodes = np.cos(np.linspace(0, np.pi, 4000)) * 0.25
    square = nodes * nodes
    basis = np.stack([nodes * square**i for i in range(terms)], 1)
    found = np.linalg.lstsq(basis, np.sin(2 * np.pi * nodes), rcond=None)[0]
    return [float(np.float32(value)) for value in found]


SIN = fit_sine(4)
TURN = 0.0025 / (2.0 * math.pi)
NN = (((1,), (0,)), ((), ()))
NT = (((1,), (1,)), ((), ()))


def split(values):
    high = values.astype(bf16)
    return high, (values - high.astype(f32)).astype(bf16)


def cosine(turns):
    rest = turns - jnp.round(turns)
    place = 0.25 - jnp.abs(rest)
    square = place * place
    series = SIN[-1]
    for term in SIN[-2::-1]:
        series = series * square + term
    return series * place


def divisor(size, most):
    while size % most:
        most //= 2
    return most


def build_kernel(
    own_ref, other_ref, freq_ref, phase_ref, amp_ref, coeffs_ref, blank_high, blank_low, image_own, image_other, base_ref, high_ref, low_ref,
    freq_buf, freq_sem,
):
    paths, width = high_ref.shape
    half = paths // 2
    cols = freq_buf.shape[2]
    rows = divisor(half, 512)
    steps = width // cols
    count = coeffs_ref.shape[0]
    first = lax.axis_index("paths") * width
    image_own[...] = jnp.zeros_like(image_own)
    image_other[...] = jnp.zeros_like(image_other)

    def fetch(index, slot):
        source = pl.ds(pl.multiple_of(first + index * cols, cols), cols)
        return pltpu.make_async_copy(freq_ref.at[:, source], freq_buf.at[slot], freq_sem.at[slot])

    fetch(0, 0).start()

    def block(index, carry):
        slot = lax.rem(index, 2)

        @pl.when(index + 1 < steps)
        def _():
            fetch(index + 1, 1 - slot).start()

        fetch(index, slot).wait()
        span = pl.ds(pl.multiple_of(first + index * cols, cols), cols)
        target = pl.ds(pl.multiple_of(index * cols, cols), cols)
        freq = freq_buf[slot].astype(f32).astype(bf16)
        phase = phase_ref[:, span].astype(f32) * (1.0 / 1024.0)
        amp = amp_ref[:, span]
        base_ref[:, target] = coeffs_ref[:, span]
        start_high, start_low = split(coeffs_ref[:, span])
        start = jnp.concatenate([start_high, start_low], 0)
        for part in range(paths // rows):
            factor_ref, image_ref = (own_ref, image_own) if part * rows < half else (other_ref, image_other)
            place = pl.ds(part * rows % half, rows)
            factor = factor_ref[place, :].astype(f32).astype(bf16)
            summed = lax.dot_general(factor, freq, NN, preferred_element_type=f32)
            values = cosine(summed * TURN + phase) * amp
            high, low = split(values)
            high_ref[pl.ds(part * rows, rows), target] = high
            low_ref[pl.ds(part * rows, rows), target] = low
            main = lax.dot_general(start, high, NT, preferred_element_type=f32)
            rest = lax.dot_general(start_high, low, NT, preferred_element_type=f32)
            image_ref[:, place] += main[:count] + main[count:] + rest
        return carry

    lax.fori_loop(0, steps, block, 0)


def turn_kernel(weight, own_ref, other_ref, high_ref, low_ref, *refs):
    if weight is None:
        image_own, image_other, grad_ref, pair_ref = refs
    else:
        base_ref, before_ref, scale_ref, image_own, image_other, grad_ref, base_out, pair_ref = refs
    paths, width = high_ref.shape
    half = paths // 2
    count = own_ref.shape[0]
    cols = divisor(width, 1024)
    clip_high, clip_low = split(jnp.concatenate([own_ref[...], other_ref[...]], 1))
    clip_pair = jnp.concatenate([clip_high, clip_low], 0)
    squares = jnp.zeros((8, 128), f32)
    for index in range(width // cols):
        span = pl.ds(index * cols, cols)
        main = lax.dot_general(clip_pair, high_ref[:, span], NN, preferred_element_type=f32)
        rest = lax.dot_general(clip_high, low_ref[:, span], NN, preferred_element_type=f32)
        grad = main[:count] + main[count:] + rest
        grad_ref[:, span] = grad
        high, low = split(grad)
        pair_ref[:count, span] = high
        pair_ref[count:, span] = low
        for row in range(0, count, 8):
            for lane in range(0, cols, 128):
                tile = grad[row : row + 8, lane : lane + 128]
                squares = squares + tile * tile
        if weight is not None:
            base_out[:, span] = base_ref[:, span] - weight * (before_ref[:, span] / scale_ref[0:1, 0:1])
    for image_ref, start in ((image_own, 0), (image_other, half)):
        place = pl.ds(start, half)
        main = lax.dot_general(pair_ref[...], high_ref[place, :], NT, preferred_element_type=f32)
        rest = lax.dot_general(pair_ref[:count, :], low_ref[place, :], NT, preferred_element_type=f32)
        image = main[:count] + main[count:] + rest
        for lane in range(0, half, 128):
            image_ref[pl.ds(lane // 128 * count, count), :] = image[:, lane : lane + 128]
        image_ref[pl.ds(half // 128 * count, 8), :] = squares


def add_kernel(one_ref, other_ref, sum_ref):
    sum_ref[...] = one_ref[...] + other_ref[...]


def open_kernel(sum_ref, last_ref, targets_ref, clipped_out, predicted_out):
    predicted = sum_ref[...] + last_ref[...]
    predicted_out[...] = predicted
    clipped_out[...] = jnp.clip(predicted - targets_ref[...], -huber_cap, huber_cap)


def step_kernel(entries, sum_ref, last_ref, targets_ref, predicted_ref, *refs):
    if len(refs) == 5:
        tracked_ref = refs[0]
        refs = refs[1:]
    else:
        tracked_ref = None
    clipped_out, predicted_out, scale_out, tracked_out = refs
    count, half = targets_ref.shape
    tiles = half // 128
    end = pl.ds(tiles * count, 8)
    total = jnp.sum(sum_ref[end, :] + last_ref[end, :], axis=(0, 1), keepdims=True)
    scale = jnp.sqrt(total / entries + epsilon)
    scale_out[...] = jnp.broadcast_to(scale, (8, 128))
    for tile in range(tiles):
        place, span = pl.ds(tile * count, count), pl.ds(tile * 128, 128)
        tracked = (sum_ref[place, :] + last_ref[place, :]) / scale
        if tracked_ref is not None:
            tracked = momentum * tracked_ref[:, span] + tracked
        predicted = predicted_ref[:, span] - step_rate * tracked
        tracked_out[:, span] = tracked
        predicted_out[:, span] = predicted
        clipped_out[:, span] = jnp.clip(predicted - targets_ref[:, span], -huber_cap, huber_cap)


def close_kernel(weight, base_ref, other_base, grad_ref, other_grad, scale_ref, coeffs_out):
    width = base_ref.shape[1]
    core = lax.axis_index("paths")
    scale = scale_ref[0:1, 0:1]
    for start, base, grad in ((core, base_ref, grad_ref), (1 - core, other_base, other_grad)):
        span = pl.ds(pl.multiple_of(start * width, width), width)
        coeffs_out[:, span] = base[...] - weight * (grad[...] / scale)


def vmem(count):
    return [pl.BlockSpec(memory_space=pltpu.VMEM)] * count


def hbm(count):
    return [pl.BlockSpec(memory_space=pl.ANY)] * count


def held(array):
    return pltpu.with_memory_space_constraint(array, pltpu.VMEM)


def call(kernel, name, arguments, shapes, specs=None, scratch=(), megabytes=4, aliases={}):
    shapes = tuple(shape if not isinstance(shape, tuple) else jax.ShapeDtypeStruct(shape, f32) for shape in shapes)
    return pl.pallas_call(
        kernel,
        out_shape=shapes,
        in_specs=specs or vmem(len(arguments)),
        out_specs=tuple(vmem(len(shapes))),
        scratch_shapes=scratch,
        compiler_params=pltpu.CompilerParams(vmem_limit_bytes=megabytes * 2**20),
        input_output_aliases=aliases,
        name=name,
    )(*arguments)


def shards(sizes, factors, frequency, phases, amplitude, targets, coeffs_init):
    cores, chips = sizes["paths"], sizes["feats"]
    half = factors.shape[0]
    width = frequency.shape[1] // cores
    count = targets.shape[0]
    paths = half * cores
    entries = count * width * cores * chips
    hops = [1 << bit for bit in range(chips.bit_length() - 1)]

    def swap(array):
        return lax.ppermute(array, "paths", [(0, 1), (1, 0)])

    def add(one, other):
        return call(add_kernel, "add", (one, other), (one.shape,))[0]

    def all_chips(array):
        for step in range(len(hops)):
            pairs = [
                (way * chips + chip, way * chips + (chip ^ hops[(step + way) % len(hops)]))
                for way in range(cores)
                for chip in range(chips)
            ]
            last = lax.ppermute(array, ("paths", "feats"), pairs)
            if step < len(hops) - 1:
                array = add(array, last)
        return array, last

    cols = divisor(width, 512)
    small, wide = (count, half), (count, width)
    blanks = [
        pl.pallas_call(
            lambda out: None,
            out_shape=pltpu.VMEM((paths, width), bf16),
            out_specs=vmem(1)[0],
            compiler_params=pltpu.CompilerParams(vmem_limit_bytes=2**20),
            name=name,
        )()
        for name in ("blank_high", "blank_low")
    ]
    blank_high, blank_low = blanks
    image_own, image_other, base, high, low = call(
        build_kernel,
        "build",
        (factors, swap(factors), frequency, phases[None], amplitude[None], coeffs_init, held(blank_high), held(blank_low)),
        (small, small, wide, pltpu.VMEM((paths, width), bf16), pltpu.VMEM((paths, width), bf16)),
        vmem(2) + hbm(1) + vmem(5),
        [pltpu.VMEM((2,) + (frequency.shape[0], cols), frequency.dtype), pltpu.SemaphoreType.DMA((2,))],
        20,
        {6: 3, 7: 4},
    )
    array, last = all_chips(add(image_own, swap(image_other)))
    clipped, predicted = call(open_kernel, "open", (array, last, targets), (small, small))
    extent = (count * half // 128 + 8, 128)
    weights = [step_rate * sum(momentum**later for later in range(ITERS - turn)) for turn in range(ITERS)]
    tracked = ()
    for turn in range(ITERS):
        arguments = (clipped, swap(clipped), held(high), held(low))
        shapes = (extent, extent, wide)
        if turn:
            arguments += (base, grad, scale)
            shapes += (wide,)
        image_own, image_other, grad, *rest = call(
            functools.partial(turn_kernel, weights[turn - 1] if turn else None),
            "turn",
            arguments,
            shapes,
            None,
            [pltpu.VMEM((2 * count, width), bf16)],
            20,
        )
        if turn:
            base = rest[0]
        array, last = all_chips(add(image_own, swap(image_other)))
        clipped, predicted, scale, *tracked = call(
            functools.partial(step_kernel, entries),
            "step",
            (array, last, targets, predicted, *tracked),
            (small, small, (8, 128), small),
        )
    coeffs = call(
        functools.partial(close_kernel, weights[-1]),
        "close",
        (base, swap(base), grad, swap(grad), scale),
        ((count, width * cores),),
        None,
        (),
        8,
    )[0]
    return (coeffs, predicted)


def solution(mesh):
    return jax.shard_map(
        functools.partial(shards, dict(mesh.shape)),
        mesh=mesh,
        in_specs=(
            P(("groups", "paths"), None),
            P(None, "feats"),
            P("feats"),
            P("feats"),
            P(None, ("groups", "paths")),
            P(None, ("groups", "feats")),
        ),
        out_specs=(P(None, ("groups", "feats")), P(None, ("groups", "paths"))),
        check_vma=False,
    )
```

time: 758 us -> 170 us (0.22)
  matrix products: 369 us -> 0 us
  waiting for transfers between devices: 287 us -> 53.3 us
  Pallas kernels: 0 us -> 83.1 us
  blocking collectives: 67.5 us -> 0 us
  starting transfers between devices: 0.87 us -> 29.3 us
  between operations: 16.5 us -> 1.26 us
  other arithmetic: 9.95 us -> 0 us
    dot_general x8 -> x0, matrix products: 369 us -> none  [the longest x4 145 us: image_of(): lax.dot_general(coeffs, block, (((1,), (1,)), ((), ())), precision=lax.Pr...]
    psum x7 -> x0, waiting for transfers between devices: 287 us -> none  [the longest x3 158 us: shards(): lax.psum((image_of(gradient, block), jnp.sum(gradient * gradient)), 'feats')]
    pallas_call x0 -> x23, Pallas kernels: none -> 83.1 us  [the longest x21 83.1 us: call(): pl.pallas_call(kernel, out_shape=shapes, in_specs=specs or vmem(len(argum...]
    psum x3 -> x0, blocking collectives: 67.5 us -> none  [shards(): lax.psum((image_of(gradient, block), jnp.sum(gradient * gradient)), 'feats')]
    ppermute x0 -> x22, waiting for transfers between devices: none -> 53.3 us  [the longest x12 43.5 us: all_chips(): last = lax.ppermute(array, ('paths', 'feats'), pairs)]
    ppermute x0 -> x22, starting transfers between devices: none -> 29.3 us  [the longest x12 27.1 us: all_chips(): last = lax.ppermute(array, ('paths', 'feats'), pairs)]
  transfers between devices with their start and end apart: 7 -> 22, of which waited for: 7 -> 20; matrix products, arithmetic and copies ran while one was open for 1% -> 0% of each run, Pallas kernels for 0% -> 1%
where the time goes in v1:
time: 170 us; the launch traced here: 167 us
  Pallas kernels  83.1 us (49%)
  waiting for transfers between devices  53.3 us (31%)
  starting transfers between devices  29.3 us (17%)
    pallas_call x21, Pallas kernels, call(): pl.pallas_call(kernel, out_shape=shapes, in_specs=specs or vmem(len(argum...  83.1 us
    ppermute x12, waiting for transfers between devices, all_chips(): last = lax.ppermute(array, ('paths', 'feats'), pairs)  43.5 us
    ppermute x12, starting transfers between devices, all_chips(): last = lax.ppermute(array, ('paths', 'feats'), pairs)  27.1 us
    ppermute x10, waiting for transfers between devices, swap(): return lax.ppermute(array, 'paths', [(0, 1), (1, 0)])  9.85 us
  transfers between devices with their start and end apart: 22, of which 20 were waited for; matrix products, arithmetic and copies ran while one was open for 0% of the time, Pallas kernels for 1%

profile of v1, /device:TPU:0, one launch (start us, length us, event | category | flops | bytes accessed | tf_op | source)
XLA Modules:
  0.0 167.1 jit_solution(6309314372492480874)
XLA Ops:
  1.2 1.7 %collective-permute-done.other_ref = s32[1024,128]{1,0:T(8,128)S(1)} collective-permute-done((s32[1024,128]{1,0:T(8,128)}, s32[1024,128]{1,0:T(8,128)S(1)}, u32[]{:S(2)}, u32[]{:S(2)}) %collective-permute-start) | collective-permute-done | bytes 524320 | tf_op jit(solution)/shard_map/ppermute | solution.py:230
  2.9 30.3 %build.1 = (f32[32,1024]{1,0:T(8,128)S(1)}, f32[32,1024]{1,0:T(8,128)S(1)}, f32[32,4096]{1,0:T(8,128)S(1)}, bf16[2048,4096]{1,0:T(8,128)(2,1)S(1)}, bf16[2048,4096]{1,0:T(8,128)(2,1)S(1)}) custom-call(s32[1024,128]{1,0:T(8,128)S(1)} %copy-done.1, s32[1024,128]{1,0:T(8,128)S(1)} %collective-permute-done.other_ref, ...), custom_call_target="tpu_custom_call", output_to_operand_aliasing={{3}: (6, {}), {4}: (7, {})} | custom-call | tf_op jit(solution)/shard_map/build/pallas_call | solution.py:208
  34.7 2.9 %collective-permute-start.2 = (f32[32,1024]{1,0:T(8,128)S(1)}, f32[32,1024]{1,0:T(8,128)S(1)}, u32[]{:S(2)}, u32[]{:S(2)}) collective-permute-start(f32[32,1024]{1,0:T(8,128)S(1)} %add.12.one_ref), channel_id=1, source_target_pairs={{0,1},{1,0},{2,3},{3,2},{4,5},{5,4},{6,7},{7,6},{8,10},{9,11},{10,... | collective-permute-start | bytes 393224 | tf_op jit(solution)/shard_map/ppermute | solution.py:242
  37.7 2.9 %collective-permute-done.2.other_ref = f32[32,1024]{1,0:T(8,128)S(1)} collective-permute-done((f32[32,1024]{1,0:T(8,128)S(1)}, f32[32,1024]{1,0:T(8,128)S(1)}, u32[]{:S(2)}, u32[]{:S(2)}) %collective-permute-start.2) | collective-permute-done | bytes 131104 | tf_op jit(solution)/shard_map/ppermute | solution.py:242
  40.7 2.1 %collective-permute-start.3 = (f32[32,1024]{1,0:T(8,128)S(1)}, f32[32,1024]{1,0:T(8,128)S(1)}, u32[]{:S(2)}, u32[]{:S(2)}) collective-permute-start(f32[32,1024]{1,0:T(8,128)S(1)} %add.13.one_ref), channel_id=1, source_target_pairs={{0,2},{1,3},{2,0},{3,1},{4,6},{5,7},{6,4},{7,5},{8,12},{9,13},{10,... | collective-permute-start | bytes 393224 | tf_op jit(solution)/shard_map/ppermute | solution.py:242
  42.8 3.7 %collective-permute-done.3.other_ref = f32[32,1024]{1,0:T(8,128)S(1)} collective-permute-done((f32[32,1024]{1,0:T(8,128)S(1)}, f32[32,1024]{1,0:T(8,128)S(1)}, u32[]{:S(2)}, u32[]{:S(2)}) %collective-permute-start.3) | collective-permute-done | bytes 131104 | tf_op jit(solution)/shard_map/ppermute | solution.py:242
  46.5 2.7 %collective-permute-start.4 = (f32[32,1024]{1,0:T(8,128)S(1)}, f32[32,1024]{1,0:T(8,128)S(1)}, u32[]{:S(2)}, u32[]{:S(2)}) collective-permute-start(f32[32,1024]{1,0:T(8,128)S(1)} %add.14.sum_ref), channel_id=1, source_target_pairs={{0,4},{1,5},{2,6},{3,7},{4,0},{5,1},{6,2},{7,3},{8,9},{9,8},{10,11... | collective-permute-start | bytes 393224 | tf_op jit(solution)/shard_map/ppermute | solution.py:242
  49.2 3.3 %collective-permute-done.4.last_ref = f32[32,1024]{1,0:T(8,128)S(1)} collective-permute-done((f32[32,1024]{1,0:T(8,128)S(1)}, f32[32,1024]{1,0:T(8,128)S(1)}, u32[]{:S(2)}, u32[]{:S(2)}) %collective-permute-start.4) | collective-permute-done | bytes 131104 | tf_op jit(solution)/shard_map/ppermute | solution.py:242
  52.6 1.3 collective-permute-done.5.other_ref
  53.9 15.8 %turn.3 = (f32[264,128]{1,0:T(8,128)S(1)}, f32[264,128]{1,0:T(8,128)S(1)}, f32[32,4096]{1,0:T(8,128)S(1)}) custom-call(f32[32,1024]{1,0:T(8,128)S(1)} %get-tuple-element.32.own_ref, f32[32,1024]{1,0:T(8,128)S(1)} %collective-permute-done.5.other_ref, bf16[2048,4096]{1,0:T(8,128)(2,1)S(1)} %get-tuple-element.33.high_ref, ...), custom_call_target="tpu_custom_call" | custom-call | tf_op jit(solution)/shard_map/turn/pallas_call | solution.py:208
  71.1 1.6 collective-permute-start.7
  72.7 3.5 %collective-permute-done.7.other_ref = f32[264,128]{1,0:T(8,128)S(1)} collective-permute-done((f32[264,128]{1,0:T(8,128)S(1)}, f32[264,128]{1,0:T(8,128)S(1)}, u32[]{:S(2)}, u32[]{:S(2)}) %collective-permute-start.7) | collective-permute-done | bytes 135200 | tf_op jit(solution)/shard_map/ppermute | solution.py:242
  76.2 2.2 %collective-permute-start.8 = (f32[264,128]{1,0:T(8,128)S(1)}, f32[264,128]{1,0:T(8,128)S(1)}, u32[]{:S(2)}, u32[]{:S(2)}) collective-permute-start(f32[264,128]{1,0:T(8,128)S(1)} %add.16.one_ref), channel_id=1, source_target_pairs={{0,2},{1,3},{2,0},{3,1},{4,6},{5,7},{6,4},{7,5},{8,12},{9,13},{10,... | collective-permute-start | bytes 405512 | tf_op jit(solution)/shard_map/ppermute | solution.py:242
  78.5 4.3 %collective-permute-done.8.other_ref = f32[264,128]{1,0:T(8,128)S(1)} collective-permute-done((f32[264,128]{1,0:T(8,128)S(1)}, f32[264,128]{1,0:T(8,128)S(1)}, u32[]{:S(2)}, u32[]{:S(2)}) %collective-permute-start.8) | collective-permute-done | bytes 135200 | tf_op jit(solution)/shard_map/ppermute | solution.py:242
  82.8 2.6 %collective-permute-start.9 = (f32[264,128]{1,0:T(8,128)S(1)}, f32[264,128]{1,0:T(8,128)S(1)}, u32[]{:S(2)}, u32[]{:S(2)}) collective-permute-start(f32[264,128]{1,0:T(8,128)S(1)} %add.17.sum_ref), channel_id=1, source_target_pairs={{0,4},{1,5},{2,6},{3,7},{4,0},{5,1},{6,2},{7,3},{8,9},{9,8},{10,11... | collective-permute-start | bytes 405512 | tf_op jit(solution)/shard_map/ppermute | solution.py:242
  85.5 3.4 %collective-permute-done.9.last_ref = f32[264,128]{1,0:T(8,128)S(1)} collective-permute-done((f32[264,128]{1,0:T(8,128)S(1)}, f32[264,128]{1,0:T(8,128)S(1)}, u32[]{:S(2)}, u32[]{:S(2)}) %collective-permute-start.9) | collective-permute-done | bytes 135200 | tf_op jit(solution)/shard_map/ppermute | solution.py:242
  89.1 1.3 collective-permute-done.10.other_ref
  90.4 17.2 %turn.4 = (f32[264,128]{1,0:T(8,128)S(1)}, f32[264,128]{1,0:T(8,128)S(1)}, f32[32,4096]{1,0:T(8,128)S(1)}, f32[32,4096]{1,0:T(8,128)S(1)}) custom-call(f32[32,1024]{1,0:T(8,128)S(1)} %get-tuple-element.38.own_ref, f32[32,1024]{1,0:T(8,128)S(1)} %collective-permute-done.10.other_ref, bf16[2048,4096]{1,0:T(8,128)(2,1)S(1)} %get-tuple-element.33.high_ref, ...), custom_call_target="tpu_custom_call" | custom-call | tf_op jit(solution)/shard_map/turn/pallas_call | solution.py:208
  109.0 1.6 collective-permute-start.12
  110.6 3.5 %collective-permute-done.12.other_ref = f32[264,128]{1,0:T(8,128)S(1)} collective-permute-done((f32[264,128]{1,0:T(8,128)S(1)}, f32[264,128]{1,0:T(8,128)S(1)}, u32[]{:S(2)}, u32[]{:S(2)}) %collective-permute-start.12) | collective-permute-done | bytes 135200 | tf_op jit(solution)/shard_map/ppermute | solution.py:242
  114.1 2.2 %collective-permute-start.13 = (f32[264,128]{1,0:T(8,128)S(1)}, f32[264,128]{1,0:T(8,128)S(1)}, u32[]{:S(2)}, u32[]{:S(2)}) collective-permute-start(f32[264,128]{1,0:T(8,128)S(1)} %add.19.one_ref), channel_id=1, source_target_pairs={{0,2},{1,3},{2,0},{3,1},{4,6},{5,7},{6,4},{7,5},{8,12},{9,13},{10,... | collective-permute-start | bytes 405512 | tf_op jit(solution)/shard_map/ppermute | solution.py:242
  116.3 4.4 %collective-permute-done.13.other_ref = f32[264,128]{1,0:T(8,128)S(1)} collective-permute-done((f32[264,128]{1,0:T(8,128)S(1)}, f32[264,128]{1,0:T(8,128)S(1)}, u32[]{:S(2)}, u32[]{:S(2)}) %collective-permute-start.13) | collective-permute-done | bytes 135200 | tf_op jit(solution)/shard_map/ppermute | solution.py:242
  120.7 2.6 %collective-permute-start.14 = (f32[264,128]{1,0:T(8,128)S(1)}, f32[264,128]{1,0:T(8,128)S(1)}, u32[]{:S(2)}, u32[]{:S(2)}) collective-permute-start(f32[264,128]{1,0:T(8,128)S(1)} %add.20.sum_ref), channel_id=1, source_target_pairs={{0,4},{1,5},{2,6},{3,7},{4,0},{5,1},{6,2},{7,3},{8,9},{9,8},{10,11... | collective-permute-start | bytes 405512 | tf_op jit(solution)/shard_map/ppermute | solution.py:242
  123.3 3.3 %collective-permute-done.14.last_ref = f32[264,128]{1,0:T(8,128)S(1)} collective-permute-done((f32[264,128]{1,0:T(8,128)S(1)}, f32[264,128]{1,0:T(8,128)S(1)}, u32[]{:S(2)}, u32[]{:S(2)}) %collective-permute-start.14) | collective-permute-done | bytes 135200 | tf_op jit(solution)/shard_map/ppermute | solution.py:242
  126.9 1.3 collective-permute-done.15.other_ref
  128.3 17.2 %turn.5 = (f32[264,128]{1,0:T(8,128)S(1)}, f32[264,128]{1,0:T(8,128)S(1)}, f32[32,4096]{1,0:T(8,128)S(1)}, f32[32,4096]{1,0:T(8,128)S(1)}) custom-call(f32[32,1024]{1,0:T(8,128)S(1)} %get-tuple-element.46.own_ref, f32[32,1024]{1,0:T(8,128)S(1)} %collective-permute-done.15.other_ref, bf16[2048,4096]{1,0:T(8,128)(2,1)S(1)} %get-tuple-element.33.high_ref, ...), custom_call_target="tpu_custom_call" | custom-call | tf_op jit(solution)/shard_map/turn/pallas_call | solution.py:208
  146.9 1.6 collective-permute-start.19
  148.4 3.5 %collective-permute-done.19.other_ref = f32[264,128]{1,0:T(8,128)S(1)} collective-permute-done((f32[264,128]{1,0:T(8,128)S(1)}, f32[264,128]{1,0:T(8,128)S(1)}, u32[]{:S(2)}, u32[]{:S(2)}) %collective-permute-start.19) | collective-permute-done | bytes 135200 | tf_op jit(solution)/shard_map/ppermute | solution.py:242
  152.0 2.2 %collective-permute-start.20 = (f32[264,128]{1,0:T(8,128)S(1)}, f32[264,128]{1,0:T(8,128)S(1)}, u32[]{:S(2)}, u32[]{:S(2)}) collective-permute-start(f32[264,128]{1,0:T(8,128)S(1)} %add.22.one_ref), channel_id=1, source_target_pairs={{0,2},{1,3},{2,0},{3,1},{4,6},{5,7},{6,4},{7,5},{8,12},{9,13},{10,... | collective-permute-start | bytes 405512 | tf_op jit(solution)/shard_map/ppermute | solution.py:242
  154.2 4.4 %collective-permute-done.20.other_ref = f32[264,128]{1,0:T(8,128)S(1)} collective-permute-done((f32[264,128]{1,0:T(8,128)S(1)}, f32[264,128]{1,0:T(8,128)S(1)}, u32[]{:S(2)}, u32[]{:S(2)}) %collective-permute-start.20) | collective-permute-done | bytes 135200 | tf_op jit(solution)/shard_map/ppermute | solution.py:242
  158.5 2.6 %collective-permute-start.21 = (f32[264,128]{1,0:T(8,128)S(1)}, f32[264,128]{1,0:T(8,128)S(1)}, u32[]{:S(2)}, u32[]{:S(2)}) collective-permute-start(f32[264,128]{1,0:T(8,128)S(1)} %add.23.sum_ref), channel_id=1, source_target_pairs={{0,4},{1,5},{2,6},{3,7},{4,0},{5,1},{6,2},{7,3},{8,9},{9,8},{10,11... | collective-permute-start | bytes 405512 | tf_op jit(solution)/shard_map/ppermute | solution.py:242
  161.2 3.3 %collective-permute-done.21.last_ref = f32[264,128]{1,0:T(8,128)S(1)} collective-permute-done((f32[264,128]{1,0:T(8,128)S(1)}, f32[264,128]{1,0:T(8,128)S(1)}, u32[]{:S(2)}, u32[]{:S(2)}) %collective-permute-start.21) | collective-permute-done | bytes 135200 | tf_op jit(solution)/shard_map/ppermute | solution.py:242
  (51 shorter events, 9.0 us)
Async XLA Ops:
  0.6 2.3 %copy-start.1 = (s32[1024,128]{1,0:T(8,128)S(1)}, s32[1024,128]{1,0:T(8,128)}, u32[]{:S(2)}) copy-start(s32[1024,128]{1,0:T(8,128)} %own_ref.1) | copy-start | bytes 1572868
  0.6 2.3 %copy-start.7 = (f32[8192]{0:T(1024)S(1)}, f32[8192]{0:T(1024)}, u32[]{:S(2)}) copy-start(f32[8192]{0:T(1024)} %param.9) | copy-start | bytes 98308
  0.6 2.3 %copy-start.6 = (s32[8192]{0:T(1024)S(1)}, s32[8192]{0:T(1024)}, u32[]{:S(2)}) copy-start(s32[8192]{0:T(1024)} %param.8) | copy-start | bytes 98308
  0.7 2.3 %collective-permute-start = (s32[1024,128]{1,0:T(8,128)}, s32[1024,128]{1,0:T(8,128)S(1)}, u32[]{:S(2)}, u32[]{:S(2)}) collective-permute-start(s32[1024,128]{1,0:T(8,128)} %own_ref.1), channel_id=1, source_target_pairs={{0,8},{8,0},{1,9},{9,1},{2,10},{10,2},{3,11},{11,3},{4,12},{12,4},... | collective-permute-start | bytes 1572872 | tf_op jit(solution)/shard_map/ppermute | solution.py:230
  2.9 49.5 %copy-start = (f32[32,1024]{1,0:T(8,128)S(1)}, f32[32,1024]{1,0:T(8,128)}, u32[]{:S(2)}) copy-start(f32[32,1024]{1,0:T(8,128)} %targets_ref.7) | copy-start | bytes 393220
  33.3 36.4 %copy-start.2 = (f32[32,4096]{1,0:T(8,128)}, f32[32,4096]{1,0:T(8,128)S(1)}, u32[]{:S(2)}) copy-start(f32[32,4096]{1,0:T(8,128)S(1)} %get-tuple-element.39.refs_0_) | copy-start | bytes 1572868
  33.3 1.4 collective-permute-start.1
  34.7 5.9 %collective-permute-start.2 = (f32[32,1024]{1,0:T(8,128)S(1)}, f32[32,1024]{1,0:T(8,128)S(1)}, u32[]{:S(2)}, u32[]{:S(2)}) collective-permute-start(f32[32,1024]{1,0:T(8,128)S(1)} %add.12.one_ref), channel_id=1, source_target_pairs={{0,1},{1,0},{2,3},{3,2},{4,5},{5,4},{6,7},{7,6},{8,10},{9,11},{10,... | collective-permute-start | bytes 393224 | tf_op jit(solution)/shard_map/ppermute | solution.py:242
  40.7 5.9 %collective-permute-start.3 = (f32[32,1024]{1,0:T(8,128)S(1)}, f32[32,1024]{1,0:T(8,128)S(1)}, u32[]{:S(2)}, u32[]{:S(2)}) collective-permute-start(f32[32,1024]{1,0:T(8,128)S(1)} %add.13.one_ref), channel_id=1, source_target_pairs={{0,2},{1,3},{2,0},{3,1},{4,6},{5,7},{6,4},{7,5},{8,12},{9,13},{10,... | collective-permute-start | bytes 393224 | tf_op jit(solution)/shard_map/ppermute | solution.py:242
  46.5 5.9 %collective-permute-start.4 = (f32[32,1024]{1,0:T(8,128)S(1)}, f32[32,1024]{1,0:T(8,128)S(1)}, u32[]{:S(2)}, u32[]{:S(2)}) collective-permute-start(f32[32,1024]{1,0:T(8,128)S(1)} %add.14.sum_ref), channel_id=1, source_target_pairs={{0,4},{1,5},{2,6},{3,7},{4,0},{5,1},{6,2},{7,3},{8,9},{9,8},{10,11... | collective-permute-start | bytes 393224 | tf_op jit(solution)/shard_map/ppermute | solution.py:242
  52.5 1.4 collective-permute-start.5
  69.7 20.7 %copy-start.5 = (f32[32,4096]{1,0:T(8,128)}, f32[32,4096]{1,0:T(8,128)S(1)}, u32[]{:S(2)}) copy-start(f32[32,4096]{1,0:T(8,128)S(1)} %get-tuple-element.40.refs_1_) | copy-start | bytes 1572868
  69.7 1.4 collective-permute-start.6
  71.1 5.1 %collective-permute-start.7 = (f32[264,128]{1,0:T(8,128)S(1)}, f32[264,128]{1,0:T(8,128)S(1)}, u32[]{:S(2)}, u32[]{:S(2)}) collective-permute-start(f32[264,128]{1,0:T(8,128)S(1)} %add.15.one_ref), channel_id=1, source_target_pairs={{0,1},{1,0},{2,3},{3,2},{4,5},{5,4},{6,7},{7,6},{8,10},{9,11},{10,... | collective-permute-start | bytes 405512 | tf_op jit(solution)/shard_map/ppermute | solution.py:242
  76.2 6.6 %collective-permute-start.8 = (f32[264,128]{1,0:T(8,128)S(1)}, f32[264,128]{1,0:T(8,128)S(1)}, u32[]{:S(2)}, u32[]{:S(2)}) collective-permute-start(f32[264,128]{1,0:T(8,128)S(1)} %add.16.one_ref), channel_id=1, source_target_pairs={{0,2},{1,3},{2,0},{3,1},{4,6},{5,7},{6,4},{7,5},{8,12},{9,13},{10,... | collective-permute-start | bytes 405512 | tf_op jit(solution)/shard_map/ppermute | solution.py:242
  82.8 6.0 %collective-permute-start.9 = (f32[264,128]{1,0:T(8,128)S(1)}, f32[264,128]{1,0:T(8,128)S(1)}, u32[]{:S(2)}, u32[]{:S(2)}) collective-permute-start(f32[264,128]{1,0:T(8,128)S(1)} %add.17.sum_ref), channel_id=1, source_target_pairs={{0,4},{1,5},{2,6},{3,7},{4,0},{5,1},{6,2},{7,3},{8,9},{9,8},{10,11... | collective-permute-start | bytes 405512 | tf_op jit(solution)/shard_map/ppermute | solution.py:242
  89.0 1.4 collective-permute-start.10
  107.6 19.3 %copy-start.3 = (f32[32,4096]{1,0:T(8,128)}, f32[32,4096]{1,0:T(8,128)S(1)}, u32[]{:S(2)}) copy-start(f32[32,4096]{1,0:T(8,128)S(1)} %get-tuple-element.48.refs_1_) | copy-start | bytes 1572868
  107.6 19.3 %copy-start.4 = (f32[32,4096]{1,0:T(8,128)}, f32[32,4096]{1,0:T(8,128)S(1)}, u32[]{:S(2)}) copy-start(f32[32,4096]{1,0:T(8,128)S(1)} %get-tuple-element.47.refs_0_) | copy-start | bytes 1572868
  107.6 1.4 collective-permute-start.11
  109.0 5.1 %collective-permute-start.12 = (f32[264,128]{1,0:T(8,128)S(1)}, f32[264,128]{1,0:T(8,128)S(1)}, u32[]{:S(2)}, u32[]{:S(2)}) collective-permute-start(f32[264,128]{1,0:T(8,128)S(1)} %add.18.one_ref), channel_id=1, source_target_pairs={{0,1},{1,0},{2,3},{3,2},{4,5},{5,4},{6,7},{7,6},{8,10},{9,11},{10,... | collective-permute-start | bytes 405512 | tf_op jit(solution)/shard_map/ppermute | solution.py:242
  114.1 6.5 %collective-permute-start.13 = (f32[264,128]{1,0:T(8,128)S(1)}, f32[264,128]{1,0:T(8,128)S(1)}, u32[]{:S(2)}, u32[]{:S(2)}) collective-permute-start(f32[264,128]{1,0:T(8,128)S(1)} %add.19.one_ref), channel_id=1, source_target_pairs={{0,2},{1,3},{2,0},{3,1},{4,6},{5,7},{6,4},{7,5},{8,12},{9,13},{10,... | collective-permute-start | bytes 405512 | tf_op jit(solution)/shard_map/ppermute | solution.py:242
  120.7 6.0 %collective-permute-start.14 = (f32[264,128]{1,0:T(8,128)S(1)}, f32[264,128]{1,0:T(8,128)S(1)}, u32[]{:S(2)}, u32[]{:S(2)}) collective-permute-start(f32[264,128]{1,0:T(8,128)S(1)} %add.20.sum_ref), channel_id=1, source_target_pairs={{0,4},{1,5},{2,6},{3,7},{4,0},{5,1},{6,2},{7,3},{8,9},{9,8},{10,11... | collective-permute-start | bytes 405512 | tf_op jit(solution)/shard_map/ppermute | solution.py:242
  126.9 1.4 collective-permute-start.15
  145.5 1.4 collective-permute-start.18
  145.6 19.8 %collective-permute-start.16 = (f32[32,4096]{1,0:T(8,128)S(1)}, f32[32,4096]{1,0:T(8,128)S(1)}, u32[]{:S(2)}, u32[]{:S(2)}) collective-permute-start(f32[32,4096]{1,0:T(8,128)S(1)} %get-tuple-element.50.base_ref), channel_id=1, source_target_pairs={{0,8},{8,0},{1,9},{9,1},{2,10},{10,2},{3,11},{11,3},{4,12},{12,4},... | collective-permute-start | bytes 1572872 | tf_op jit(solution)/shard_map/ppermute | solution.py:230
  146.0 19.4 %collective-permute-start.17 = (f32[32,4096]{1,0:T(8,128)S(1)}, f32[32,4096]{1,0:T(8,128)S(1)}, u32[]{:S(2)}, u32[]{:S(2)}) collective-permute-start(f32[32,4096]{1,0:T(8,128)S(1)} %get-tuple-element.51.grad_ref), channel_id=1, source_target_pairs={{0,8},{8,0},{1,9},{9,1},{2,10},{10,2},{3,11},{11,3},{4,12},{12,4},... | collective-permute-start | bytes 1572872 | tf_op jit(solution)/shard_map/ppermute | solution.py:230
  146.9 5.1 %collective-permute-start.19 = (f32[264,128]{1,0:T(8,128)S(1)}, f32[264,128]{1,0:T(8,128)S(1)}, u32[]{:S(2)}, u32[]{:S(2)}) collective-permute-start(f32[264,128]{1,0:T(8,128)S(1)} %add.21.one_ref), channel_id=1, source_target_pairs={{0,1},{1,0},{2,3},{3,2},{4,5},{5,4},{6,7},{7,6},{8,10},{9,11},{10,... | collective-permute-start | bytes 405512 | tf_op jit(solution)/shard_map/ppermute | solution.py:242
  152.0 6.6 %collective-permute-start.20 = (f32[264,128]{1,0:T(8,128)S(1)}, f32[264,128]{1,0:T(8,128)S(1)}, u32[]{:S(2)}, u32[]{:S(2)}) collective-permute-start(f32[264,128]{1,0:T(8,128)S(1)} %add.22.one_ref), channel_id=1, source_target_pairs={{0,2},{1,3},{2,0},{3,1},{4,6},{5,7},{6,4},{7,5},{8,12},{9,13},{10,... | collective-permute-start | bytes 405512 | tf_op jit(solution)/shard_map/ppermute | solution.py:242
  158.5 6.0 %collective-permute-start.21 = (f32[264,128]{1,0:T(8,128)S(1)}, f32[264,128]{1,0:T(8,128)S(1)}, u32[]{:S(2)}, u32[]{:S(2)}) collective-permute-start(f32[264,128]{1,0:T(8,128)S(1)} %add.23.sum_ref), channel_id=1, source_target_pairs={{0,4},{1,5},{2,6},{3,7},{4,0},{5,1},{6,2},{7,3},{8,9},{9,8},{10,11... | collective-permute-start | bytes 405512 | tf_op jit(solution)/shard_map/ppermute | solution.py:242

commit v2 on v1

v2 whole, which is shorter than its diff:
```python
import functools
import math

import jax
import jax.numpy as jnp
import numpy as np
from jax import lax
from jax.experimental import pallas as pl
from jax.experimental.pallas import tpu as pltpu
from jax.sharding import PartitionSpec as P

ITERS = 3

huber_cap = 1.0
step_rate = 0.2
momentum = 0.9
epsilon = 1e-06

f32 = jnp.float32
bf16 = jnp.bfloat16
f8 = jnp.float8_e4m3fn
NN = (((1,), (0,)), ((), ()))
NT = (((1,), (1,)), ((), ()))
TURN = 0.0025 / (2.0 * math.pi)


def fit_sine(terms):
    nodes = np.cos(np.linspace(0, np.pi, 4000)) * 0.25
    square = nodes * nodes
    basis = np.stack([nodes * square**i for i in range(terms)], 1)
    return np.linalg.lstsq(basis, np.sin(2 * np.pi * nodes), rcond=None)[0]


SINE = fit_sine(4)
TOP = float(SINE[-1])
SERIES = [float(term / SINE[-1]) for term in SINE]
LOW = 2.0**22
CLIP = 256.0


def split(values):
    high = values.astype(bf16)
    return high, (values - high.astype(f32)).astype(bf16)


def cosine(turns):
    place = 0.25 - jnp.abs(turns - jnp.round(turns))
    square = place * place
    series = square + SERIES[-2]
    for term in SERIES[-3::-1]:
        series = series * square + term
    return series * place


def divisor(size, most):
    while size % most:
        most //= 2
    return most


def build_kernel(
    own_ref, other_ref, freq_ref, phase_ref, amp_ref, coeffs_ref, blank_high, blank_low,
    image_own, image_other, amp_out, high_ref, low_ref,
    factor_buf, freq_buf, freq_sem,
):
    paths, width = high_ref.shape
    half = paths // 2
    risks = freq_buf.shape[1]
    cols = freq_buf.shape[2]
    rows = divisor(half, 512)
    steps = width // cols
    count = coeffs_ref.shape[0]
    first = lax.axis_index("paths") * width

    def fetch(index, slot):
        source = pl.ds(pl.multiple_of(first + index * cols, cols), cols)
        return pltpu.make_async_copy(freq_ref.at[:, source], freq_buf.at[slot], freq_sem.at[slot])

    fetch(0, 0).start()
    image_own[...] = jnp.zeros_like(image_own)
    image_other[...] = jnp.zeros_like(image_other)
    extra = factor_buf.shape[1] - risks
    ones = (lax.broadcasted_iota(jnp.int32, (half, extra), 1) < 3).astype(f32).astype(bf16)
    for start, ref in ((0, own_ref), (half, other_ref)):
        factor_buf[pl.ds(start, half), :risks] = ref[...].astype(f32).astype(bf16)
        factor_buf[pl.ds(start, half), risks:] = ones

    def block(index, carry):
        slot = lax.rem(index, 2)

        @pl.when(index + 1 < steps)
        def _():
            fetch(index + 1, 1 - slot).start()

        fetch(index, slot).wait()
        span = pl.ds(pl.multiple_of(first + index * cols, cols), cols)
        target = pl.ds(pl.multiple_of(index * cols, cols), cols)
        freq = freq_buf[slot].astype(f32).astype(bf16)
        phase = phase_ref[:, span].astype(f32) * (1.0 / (1024.0 * TURN))
        piece_high, rest = split(phase)
        rest = phase - piece_high.astype(f32)
        piece_middle, piece_low = split(rest)
        row = lax.broadcasted_iota(jnp.int32, (extra, cols), 0)
        pieces = jnp.where(
            row == 0,
            piece_high.astype(f32),
            jnp.where(row == 1, piece_middle.astype(f32), jnp.where(row == 2, piece_low.astype(f32), 0.0)),
        ).astype(bf16)
        freq = jnp.concatenate([freq, pieces], 0)
        amp = amp_ref[:, span] * TOP
        amp_out[:, target] = amp
        coeffs = coeffs_ref[:, span]
        start_high, start_low = split(coeffs * amp)
        start = jnp.concatenate([start_high, start_low], 0)
        for part in range(paths // rows):
            place = pl.ds(part * rows, rows)
            image_ref = image_own if part * rows < half else image_other
            summed = lax.dot_general(factor_buf[place, :], freq, NN, preferred_element_type=f32)
            values = cosine(summed * TURN)
            high = values.astype(bf16)
            rest = values - high.astype(f32)
            low = rest.astype(bf16)
            high_ref[place, target] = high
            low_ref[place, target] = (rest * LOW).astype(f8)
            main = lax.dot_general(start, high, NT, preferred_element_type=f32)
            rest = lax.dot_general(start_high, low, NT, preferred_element_type=f32)
            image_ref[:, pl.ds(part * rows % half, rows)] += main[:count] + main[count:] + rest
        return carry

    lax.fori_loop(0, steps, block, 0)


def gradient_of(clipped, high_ref, low_ref, place, span):
    count = clipped.shape[0]
    pair = jnp.concatenate(split(clipped), 0)
    main = lax.dot_general(pair, high_ref[place, span], NN, preferred_element_type=f32)
    coarse = (clipped * CLIP).astype(f8)
    rest = lax.dot_general(coarse, low_ref[place, span], NN, preferred_element_type=f32)
    return main[:count] + main[count:] + rest * (1.0 / (CLIP * LOW))


def image_of(pair_ref, coarse_ref, level, high_ref, low_ref, place, image_ref):
    count = pair_ref.shape[0] // 2
    main = lax.dot_general(pair_ref[...], high_ref[place, :], NT, preferred_element_type=f32)
    rest = lax.dot_general(coarse_ref[...], low_ref[place, :], NT, preferred_element_type=f32)
    image = main[:count] + main[count:] + rest * (level * (1.0 / LOW))
    for tile in range(image.shape[1] // 128):
        image_ref[pl.ds(tile * count, count), :] = image[:, tile * 128 : tile * 128 + 128]


def own_kernel(clipped_ref, high_ref, low_ref, partial_out):
    paths, width = high_ref.shape
    cols = divisor(width, 1024)
    for index in range(width // cols):
        span = pl.ds(index * cols, cols)
        partial_out[:, span] = gradient_of(clipped_ref[...], high_ref, low_ref, pl.ds(0, paths // 2), span)


def rest_kernel(
    clipped_ref, high_ref, low_ref, partial_ref, amp_ref, grad_out, pair_out, coarse_out, image_out, notes_out
):
    paths, width = high_ref.shape
    half = paths // 2
    count = clipped_ref.shape[0]
    cols = divisor(width, 1024)
    squares = jnp.zeros((8, 128), f32)
    largest = jnp.zeros((count, 128), f32)
    for index in range(width // cols):
        span = pl.ds(index * cols, cols)
        share = gradient_of(clipped_ref[...], high_ref, low_ref, pl.ds(half, half), span)
        amp = amp_ref[:, span]
        grad = (partial_ref[:, span] + share) * amp
        grad_out[:, span] = grad
        pushed = grad * amp
        high, low = split(pushed)
        pair_out[:count, span] = high
        pair_out[count:, span] = low
        for lane in range(0, cols, 128):
            largest = jnp.maximum(largest, jnp.abs(pushed[:, lane : lane + 128]))
            for row in range(0, count, 8):
                tile = grad[row : row + 8, lane : lane + 128]
                squares = squares + tile * tile
    level = jnp.maximum(jnp.max(largest, axis=1, keepdims=True), 1e-30) * (1.0 / 240.0)
    for index in range(width // cols):
        span = pl.ds(index * cols, cols)
        coarse_out[:, span] = (pair_out[:count, span].astype(f32) * (1.0 / level)).astype(f8)
    image_of(pair_out, coarse_out, level, high_ref, low_ref, pl.ds(half, half), image_out)
    image_out[pl.ds(count * half // 128, 8), :] = squares
    notes_out[:8, :] = squares
    notes_out[8:, :] = jnp.broadcast_to(level, (count, 128))


def image_kernel(pair_ref, coarse_ref, notes_ref, high_ref, low_ref, image_out):
    half = high_ref.shape[0] // 2
    image_of(pair_ref, coarse_ref, notes_ref[8:, :1], high_ref, low_ref, pl.ds(0, half), image_out)
    image_out[pl.ds(pair_ref.shape[0] // 2 * half // 128, 8), :] = notes_ref[:8, :]


def start_kernel(own_ref, other_ref, front_out, back_out):
    count, half = own_ref.shape
    tiles = half // 128
    for tile in range(tiles):
        out = front_out if tile < tiles // 2 else back_out
        span = pl.ds(tile * 128, 128)
        out[pl.ds(tile % (tiles // 2) * count, count), :] = own_ref[:, span] + other_ref[:, span]


def join_kernel(own_ref, other_ref, front_out, back_out):
    middle, end = back_out.shape[0], 2 * back_out.shape[0]
    front_out[:middle, :] = own_ref[:middle, :] + other_ref[:middle, :]
    front_out[middle:, :] = own_ref[end:, :] + other_ref[end:, :]
    back_out[...] = own_ref[middle:end, :] + other_ref[middle:end, :]


def add_kernel(one_ref, other_ref, sum_ref):
    sum_ref[...] = one_ref[...] + other_ref[...]


def places(targets_ref, front, back):
    count, half = targets_ref.shape
    tiles = half // 128
    for tile in range(tiles):
        refs = front if tile < tiles // 2 else back
        yield pl.ds(tile * 128, 128), refs, pl.ds(tile % (tiles // 2) * count, count)


def open_kernel(front, front_last, back, back_last, targets_ref, clipped_out, predicted_out):
    for span, (one, other), rows in places(targets_ref, (front, front_last), (back, back_last)):
        predicted = one[rows, :] + other[rows, :]
        predicted_out[:, span] = predicted
        clipped_out[:, span] = jnp.clip(predicted - targets_ref[:, span], -huber_cap, huber_cap)


def step_kernel(entries, front, front_last, back, back_last, targets_ref, predicted_ref, *refs):
    tracked_ref = refs[0] if len(refs) == 5 else None
    clipped_out, predicted_out, inverse_out, tracked_out = refs[-4:]
    end = pl.ds(back.shape[0], 8)
    total = jnp.sum(front[end, :] + front_last[end, :], axis=(0, 1), keepdims=True)
    inverse = 1.0 / jnp.sqrt(total / entries + epsilon)
    inverse_out[...] = jnp.broadcast_to(inverse, (8, 128))
    for span, (one, other), rows in places(targets_ref, (front, front_last), (back, back_last)):
        tracked = (one[rows, :] + other[rows, :]) * inverse
        if tracked_ref is not None:
            tracked = momentum * tracked_ref[:, span] + tracked
        predicted = predicted_ref[:, span] - step_rate * tracked
        tracked_out[:, span] = tracked
        predicted_out[:, span] = predicted
        clipped_out[:, span] = jnp.clip(predicted - targets_ref[:, span], -huber_cap, huber_cap)


def sum_kernel(weights, *refs):
    total = jnp.zeros_like(refs[-1])
    for weight, grad_ref, inverse_ref in zip(weights, refs[:-1:2], refs[1:-1:2]):
        total = total + (weight * inverse_ref[0:1, 0:1]) * grad_ref[...]
    refs[-1][...] = total


def close_kernel(weight, coeffs_ref, taken_ref, other_taken, grad_ref, other_grad, inverse_ref, coeffs_out):
    width = taken_ref.shape[1]
    core = lax.axis_index("paths")
    factor = weight * inverse_ref[0:1, 0:1]
    for start, taken, grad in ((core, taken_ref, grad_ref), (1 - core, other_taken, other_grad)):
        span = pl.ds(pl.multiple_of(start * width, width), width)
        coeffs_out[:, span] = coeffs_ref[:, span] - (taken[...] + factor * grad[...])


def vmem(count):
    return [pl.BlockSpec(memory_space=pltpu.VMEM)] * count


def held(array):
    return pltpu.with_memory_space_constraint(array, pltpu.VMEM)


def call(kernel, name, arguments, shapes, specs=None, scratch=(), megabytes=4, aliases={}):
    shapes = tuple(shape if not isinstance(shape, tuple) else jax.ShapeDtypeStruct(shape, f32) for shape in shapes)
    return pl.pallas_call(
        kernel,
        out_shape=shapes,
        in_specs=specs or vmem(len(arguments)),
        out_specs=tuple(vmem(len(shapes))),
        scratch_shapes=scratch,
        compiler_params=pltpu.CompilerParams(vmem_limit_bytes=megabytes * 2**20),
        input_output_aliases=aliases,
        name=name,
    )(*arguments)


def shards(sizes, factors, frequency, phases, amplitude, targets, coeffs_init):
    cores, chips = sizes["paths"], sizes["feats"]
    half, risks = factors.shape
    width = frequency.shape[1] // cores
    count = targets.shape[0]
    paths = half * cores
    entries = count * width * cores * chips
    hops = [1 << bit for bit in range(chips.bit_length() - 1)]

    def swap(array):
        return lax.ppermute(array, "paths", [(0, 1), (1, 0)])

    def add(one, other):
        return call(add_kernel, "add", (one, other), (one.shape,))[0]

    def all_chips(front, back):
        orders = hops, hops[1::-1] + hops[2:]
        sums = [front, back]
        for step in range(len(hops)):
            lasts = [
                lax.ppermute(array, "feats", [(chip, chip ^ order[step]) for chip in range(chips)])
                for array, order in zip(sums, orders)
            ]
            if step < len(hops) - 1:
                sums = [add(array, last) for array, last in zip(sums, lasts)]
        return sums[0], lasts[0], sums[1], lasts[1]

    cols = divisor(width, 512)
    small, wide, row = (count, half), (count, width), (1, width)
    extent = count * half // 128
    middle = extent // 2
    features = pltpu.VMEM((paths, width), bf16), pltpu.VMEM((paths, width), f8)
    blanks = [
        pl.pallas_call(
            lambda out: None,
            out_shape=feature,
            out_specs=vmem(1)[0],
            compiler_params=pltpu.CompilerParams(vmem_limit_bytes=2**20),
            name=name,
        )()
        for name, feature in zip(("blank_high", "blank_low"), features)
    ]
    image_own, image_other, amp, high, low = call(
        build_kernel,
        "build",
        (factors, swap(factors), frequency, phases[None], amplitude[None], coeffs_init, held(blanks[0]), held(blanks[1])),
        (small, small, row, *features),
        vmem(2) + [pl.BlockSpec(memory_space=pl.ANY)] + vmem(5),
        [
            pltpu.VMEM((paths, 2 * risks), bf16),
            pltpu.VMEM((2, risks, cols), frequency.dtype),
            pltpu.SemaphoreType.DMA((2,)),
        ],
        20,
        {6: 3, 7: 4},
    )
    sums = all_chips(*call(start_kernel, "start", (image_own, swap(image_other)), ((middle, 128), (middle, 128))))
    clipped, predicted = call(open_kernel, "open", (*sums, targets), (small, small))
    weights = [step_rate * sum(momentum**later for later in range(ITERS - turn)) for turn in range(ITERS)]
    tracked = ()
    grads, inverses = [], []
    for turn in range(ITERS):
        partial = call(own_kernel, "own", (clipped, held(high), held(low)), (wide,), None, (), 20)[0]
        pieces = jax.ShapeDtypeStruct((2 * count, width), bf16), jax.ShapeDtypeStruct(wide, f8)
        grad, pair, coarse, image_other, notes = call(
            rest_kernel,
            "rest",
            (swap(clipped), held(high), held(low), partial, amp),
            (wide, *pieces, (extent + 8, 128), (count + 8, 128)),
            None,
            (),
            20,
        )
        image_own = call(
            image_kernel, "image", (pair, coarse, notes, held(high), held(low)), ((extent + 8, 128),), None, (), 20
        )[0]
        halves = call(join_kernel, "join", (image_own, swap(image_other)), ((middle + 8, 128), (middle, 128)))
        clipped, predicted, inverse, *tracked = call(
            functools.partial(step_kernel, entries),
            "step",
            (*all_chips(*halves), targets, predicted, *tracked),
            (small, small, (8, 128), small),
        )
        grads.append(grad)
        inverses.append(inverse)
    before = [array for pair in zip(grads[:-1], inverses[:-1]) for array in pair]
    taken = call(functools.partial(sum_kernel, weights[:-1]), "sum", before, (wide,))[0]
    coeffs = call(
        functools.partial(close_kernel, weights[-1]),
        "close",
        (coeffs_init, taken, swap(taken), grads[-1], swap(grads[-1]), inverses[-1]),
        ((count, width * cores),),
        None,
        (),
        8,
    )[0]
    return (coeffs, predicted)


def solution(mesh):
    return jax.shard_map(
        functools.partial(shards, dict(mesh.shape)),
        mesh=mesh,
        in_specs=(
            P(("groups", "paths"), None),
            P(None, "feats"),
            P("feats"),
            P("feats"),
            P(None, ("groups", "paths")),
            P(None, ("groups", "feats")),
        ),
        out_specs=(P(None, ("groups", "feats")), P(None, ("groups", "paths"))),
        check_vma=False,
    )
```

time: 170 us -> 138 us (0.81); the launches traced: 167 us -> 137 us
  waiting for transfers between devices: 53.3 us -> 25.7 us
  Pallas kernels: 83.1 us -> 63.8 us
  starting transfers between devices: 29.3 us -> 46.1 us
    ppermute x12 -> x24, waiting for transfers between devices: 43.5 us -> 22.6 us  [all_chips(): lax.ppermute(array, 'feats', [(chip, chip ^ order[step]) for chip in rang...]
    pallas_call x21 -> x36, Pallas kernels: 83.1 us -> 63.8 us  [call(): pl.pallas_call(kernel, out_shape=shapes, in_specs=specs or vmem(len(argum...]
    ppermute x12 -> x24, starting transfers between devices: 27.1 us -> 43.1 us  [all_chips(): lax.ppermute(array, 'feats', [(chip, chip ^ order[step]) for chip in rang...]
    ppermute x10, waiting for transfers between devices: 9.85 us -> 3.08 us  [swap(): return lax.ppermute(array, 'paths', [(0, 1), (1, 0)])]
  transfers between devices with their start and end apart: 22 -> 34, of which waited for: 20 -> 15; matrix products, arithmetic and copies ran while one was open for 0% -> 0% of each run, Pallas kernels for 1% -> 18%
where the time goes in v2:
time: 138 us; the launch traced here: 137 us
  Pallas kernels  63.8 us (46%)
  starting transfers between devices  46.1 us (33%)
  waiting for transfers between devices  25.7 us (19%)
    pallas_call x36, Pallas kernels, call(): pl.pallas_call(kernel, out_shape=shapes, in_specs=specs or vmem(len(argum...  63.8 us
    ppermute x24, starting transfers between devices, all_chips(): lax.ppermute(array, 'feats', [(chip, chip ^ order[step]) for chip in rang...  43.1 us
    ppermute x24, waiting for transfers between devices, all_chips(): lax.ppermute(array, 'feats', [(chip, chip ^ order[step]) for chip in rang...  22.6 us
    ppermute x10, waiting for transfers between devices, swap(): return lax.ppermute(array, 'paths', [(0, 1), (1, 0)])  3.08 us
    ppermute x10, starting transfers between devices, swap(): return lax.ppermute(array, 'paths', [(0, 1), (1, 0)])  2.98 us
  transfers between devices with their start and end apart: 34, of which 15 were waited for; matrix products, arithmetic and copies ran while one was open for 0% of the time, Pallas kernels for 18%

profile of v2, /device:TPU:0, one launch (start us, length us, event | category | flops | bytes accessed | tf_op | source)
XLA Modules:
  0.0 137.4 jit_solution(17446485956159978897)
XLA Ops:
  1.2 1.7 %collective-permute-done.other_ref = s32[1024,128]{1,0:T(8,128)S(1)} collective-permute-done((s32[1024,128]{1,0:T(8,128)}, s32[1024,128]{1,0:T(8,128)S(1)}, u32[]{:S(2)}, u32[]{:S(2)}) %collective-permute-start) | collective-permute-done | bytes 524320 | tf_op jit(solution)/shard_map/ppermute | solution.py:299
  3.8 25.8 %build.1 = (f32[32,1024]{1,0:T(8,128)S(1)}, f32[32,1024]{1,0:T(8,128)S(1)}, f32[1,4096]{1,0:T(1,128)S(1)}, bf16[2048,4096]{1,0:T(8,128)(2,1)S(1)}, f8e4m3fn[2048,4096]{1,0:T(32,128)(4,1)S(1)}) custom-call(s32[1024,128]{1,0:T(8,128)S(1)} %copy-done.3, s32[1024,128]{1,0:T(8,128)S(1)} %collective-permute-done.other_ref, ...), custom_call_target="tpu_custom_call", output_to_operand_aliasing={{3}: (6, {}), {4}: (7, {})} | custom-call | tf_op jit(solution)/shard_map/build/pallas_call | solution.py:277
  31.0 2.7 %collective-permute-start.2 = (f32[128,128]{1,0:T(8,128)S(1)}, f32[128,128]{1,0:T(8,128)S(1)}, u32[]{:S(2)}, u32[]{:S(2)}) collective-permute-start(f32[128,128]{1,0:T(8,128)S(1)} %get-tuple-element.44.one_ref), channel_id=1, source_target_pairs={{0,1},{1,0},{2,3},{3,2},{4,5},{5,4},{6,7},{7,6},{8,9},{9,8},{10,11... | collective-permute-start | bytes 196616 | tf_op jit(solution)/shard_map/ppermute | solution.py:309
  36.4 1.9 %collective-permute-start.3 = (f32[128,128]{1,0:T(8,128)S(1)}, f32[128,128]{1,0:T(8,128)S(1)}, u32[]{:S(2)}, u32[]{:S(2)}) collective-permute-start(f32[128,128]{1,0:T(8,128)S(1)} %add.16.one_ref), channel_id=1, source_target_pairs={{0,2},{1,3},{2,0},{3,1},{4,6},{5,7},{6,4},{7,5},{8,10},{9,11},{10,... | collective-permute-start | bytes 196616 | tf_op jit(solution)/shard_map/ppermute | solution.py:309
  38.2 1.6 %collective-permute-start.6 = (f32[128,128]{1,0:T(8,128)S(1)}, f32[128,128]{1,0:T(8,128)S(1)}, u32[]{:S(2)}, u32[]{:S(2)}) collective-permute-start(f32[128,128]{1,0:T(8,128)S(1)} %add.18.one_ref), channel_id=1, source_target_pairs={{0,1},{1,0},{2,3},{3,2},{4,5},{5,4},{6,7},{7,6},{8,9},{9,8},{10,11... | collective-permute-start | bytes 196616 | tf_op jit(solution)/shard_map/ppermute | solution.py:309
  40.7 2.9 %collective-permute-start.4 = (f32[128,128]{1,0:T(8,128)S(1)}, f32[128,128]{1,0:T(8,128)S(1)}, u32[]{:S(2)}, u32[]{:S(2)}) collective-permute-start(f32[128,128]{1,0:T(8,128)S(1)} %add.17.front), channel_id=1, source_target_pairs={{0,4},{1,5},{2,6},{3,7},{4,0},{5,1},{6,2},{7,3},{8,12},{9,13},{10,... | collective-permute-start | bytes 196616 | tf_op jit(solution)/shard_map/ppermute | solution.py:309
  43.6 1.6 %collective-permute-start.7 = (f32[128,128]{1,0:T(8,128)S(1)}, f32[128,128]{1,0:T(8,128)S(1)}, u32[]{:S(2)}, u32[]{:S(2)}) collective-permute-start(f32[128,128]{1,0:T(8,128)S(1)} %add.19.back), channel_id=1, source_target_pairs={{0,4},{1,5},{2,6},{3,7},{4,0},{5,1},{6,2},{7,3},{8,12},{9,13},{10,... | collective-permute-start | bytes 196616 | tf_op jit(solution)/shard_map/ppermute | solution.py:309
  45.2 2.8 %collective-permute-done.4.front_last = f32[128,128]{1,0:T(8,128)S(1)} collective-permute-done((f32[128,128]{1,0:T(8,128)S(1)}, f32[128,128]{1,0:T(8,128)S(1)}, u32[]{:S(2)}, u32[]{:S(2)}) %collective-permute-start.4) | collective-permute-done | bytes 65568 | tf_op jit(solution)/shard_map/ppermute | solution.py:309
  48.9 2.1 %own.3.partial_ref = f32[32,4096]{1,0:T(8,128)S(1)} custom-call(f32[32,1024]{1,0:T(8,128)S(1)} %get-tuple-element.46.clipped_ref, bf16[2048,4096]{1,0:T(8,128)(2,1)S(1)} %get-tuple-element.47.high_ref, f8e4m3fn[2048,4096]{1,0:T(32,128)(4,1)S(1)} %get-tuple-element.48.low_ref), custom_call_target="tpu_custom_call" | custom-call | tf_op jit(solution)/shard_map/own/pallas_call | solution.py:277
  51.1 5.8 %rest.3 = (f32[32,4096]{1,0:T(8,128)S(1)}, bf16[64,4096]{1,0:T(8,128)(2,1)S(1)}, f8e4m3fn[32,4096]{1,0:T(32,128)(4,1)S(1)}, f32[264,128]{1,0:T(8,128)S(1)}, f32[40,128]{1,0:T(8,128)S(1)}) custom-call(f32[32,1024]{1,0:T(8,128)S(1)} %collective-permute-done.8.clipped_ref, bf16[2048,4096]{1,0:T(8,128)(2,1)S(1)} %get-tuple-element.47.high_ref, ...), custom_call_target="tpu_custom_call" | custom-call | tf_op jit(solution)/shard_map/rest/pallas_call | solution.py:277
  57.4 3.7 %image.3.own_ref = f32[264,128]{1,0:T(8,128)S(1)} custom-call(bf16[64,4096]{1,0:T(8,128)(2,1)S(1)} %get-tuple-element.51.pair_ref, f8e4m3fn[32,4096]{1,0:T(32,128)(4,1)S(1)} %get-tuple-element.52.coarse_ref, f32[40,128]{1,0:T(8,128)S(1)} %get-tuple-element.53.notes_ref, bf16[2048,4096]{1,0:T(8,128)(2,1)S(1)} %get-tuple-element.47.high_ref, ...), custom_call_target="tpu_custom_call" | custom-call | tf_op jit(solution)/shard_map/image/pallas_call | solution.py:277
  61.1 1.6 %collective-permute-start.10 = (f32[136,128]{1,0:T(8,128)S(1)}, f32[136,128]{1,0:T(8,128)S(1)}, u32[]{:S(2)}, u32[]{:S(2)}) collective-permute-start(f32[136,128]{1,0:T(8,128)S(1)} %get-tuple-element.55.one_ref), channel_id=1, source_target_pairs={{0,1},{1,0},{2,3},{3,2},{4,5},{5,4},{6,7},{7,6},{8,9},{9,8},{10,11... | collective-permute-start | bytes 208904 | tf_op jit(solution)/shard_map/ppermute | solution.py:309
  65.5 1.6 %collective-permute-start.11 = (f32[136,128]{1,0:T(8,128)S(1)}, f32[136,128]{1,0:T(8,128)S(1)}, u32[]{:S(2)}, u32[]{:S(2)}) collective-permute-start(f32[136,128]{1,0:T(8,128)S(1)} %add.20.one_ref), channel_id=1, source_target_pairs={{0,2},{1,3},{2,0},{3,1},{4,6},{5,7},{6,4},{7,5},{8,10},{9,11},{10,... | collective-permute-start | bytes 208904 | tf_op jit(solution)/shard_map/ppermute | solution.py:309
  67.2 1.6 %collective-permute-start.14 = (f32[128,128]{1,0:T(8,128)S(1)}, f32[128,128]{1,0:T(8,128)S(1)}, u32[]{:S(2)}, u32[]{:S(2)}) collective-permute-start(f32[128,128]{1,0:T(8,128)S(1)} %add.22.one_ref), channel_id=1, source_target_pairs={{0,1},{1,0},{2,3},{3,2},{4,5},{5,4},{6,7},{7,6},{8,9},{9,8},{10,11... | collective-permute-start | bytes 196616 | tf_op jit(solution)/shard_map/ppermute | solution.py:309
  69.9 1.8 %collective-permute-start.12 = (f32[136,128]{1,0:T(8,128)S(1)}, f32[136,128]{1,0:T(8,128)S(1)}, u32[]{:S(2)}, u32[]{:S(2)}) collective-permute-start(f32[136,128]{1,0:T(8,128)S(1)} %add.21.front), channel_id=1, source_target_pairs={{0,4},{1,5},{2,6},{3,7},{4,0},{5,1},{6,2},{7,3},{8,12},{9,13},{10,... | collective-permute-start | bytes 208904 | tf_op jit(solution)/shard_map/ppermute | solution.py:309
  71.7 2.0 %collective-permute-start.15 = (f32[128,128]{1,0:T(8,128)S(1)}, f32[128,128]{1,0:T(8,128)S(1)}, u32[]{:S(2)}, u32[]{:S(2)}) collective-permute-start(f32[128,128]{1,0:T(8,128)S(1)} %add.23.back), channel_id=1, source_target_pairs={{0,4},{1,5},{2,6},{3,7},{4,0},{5,1},{6,2},{7,3},{8,12},{9,13},{10,... | collective-permute-start | bytes 196616 | tf_op jit(solution)/shard_map/ppermute | solution.py:309
  73.7 3.3 %collective-permute-done.15.back_last = f32[128,128]{1,0:T(8,128)S(1)} collective-permute-done((f32[128,128]{1,0:T(8,128)S(1)}, f32[128,128]{1,0:T(8,128)S(1)}, u32[]{:S(2)}, u32[]{:S(2)}) %collective-permute-start.15) | collective-permute-done | bytes 65568 | tf_op jit(solution)/shard_map/ppermute | solution.py:309
  77.3 2.1 %own.4.partial_ref = f32[32,4096]{1,0:T(8,128)S(1)} custom-call(f32[32,1024]{1,0:T(8,128)S(1)} %get-tuple-element.59.clipped_ref, bf16[2048,4096]{1,0:T(8,128)(2,1)S(1)} %get-tuple-element.47.high_ref, f8e4m3fn[2048,4096]{1,0:T(32,128)(4,1)S(1)} %get-tuple-element.48.low_ref), custom_call_target="tpu_custom_call" | custom-call | tf_op jit(solution)/shard_map/own/pallas_call | solution.py:277
  79.4 6.0 %rest.4 = (f32[32,4096]{1,0:T(8,128)S(1)}, bf16[64,4096]{1,0:T(8,128)(2,1)S(1)}, f8e4m3fn[32,4096]{1,0:T(32,128)(4,1)S(1)}, f32[264,128]{1,0:T(8,128)S(1)}, f32[40,128]{1,0:T(8,128)S(1)}) custom-call(f32[32,1024]{1,0:T(8,128)S(1)} %collective-permute-done.16.clipped_ref, bf16[2048,4096]{1,0:T(8,128)(2,1)S(1)} %get-tuple-element.47.high_ref, ...), custom_call_target="tpu_custom_call" | custom-call | tf_op jit(solution)/shard_map/rest/pallas_call | solution.py:277
  86.0 3.7 %image.4.own_ref = f32[264,128]{1,0:T(8,128)S(1)} custom-call(bf16[64,4096]{1,0:T(8,128)(2,1)S(1)} %get-tuple-element.61.pair_ref, f8e4m3fn[32,4096]{1,0:T(32,128)(4,1)S(1)} %get-tuple-element.62.coarse_ref, f32[40,128]{1,0:T(8,128)S(1)} %get-tuple-element.63.notes_ref, bf16[2048,4096]{1,0:T(8,128)(2,1)S(1)} %get-tuple-element.47.high_ref, ...), custom_call_target="tpu_custom_call" | custom-call | tf_op jit(solution)/shard_map/image/pallas_call | solution.py:277
  89.7 1.6 %collective-permute-start.18 = (f32[136,128]{1,0:T(8,128)S(1)}, f32[136,128]{1,0:T(8,128)S(1)}, u32[]{:S(2)}, u32[]{:S(2)}) collective-permute-start(f32[136,128]{1,0:T(8,128)S(1)} %get-tuple-element.65.one_ref), channel_id=1, source_target_pairs={{0,1},{1,0},{2,3},{3,2},{4,5},{5,4},{6,7},{7,6},{8,9},{9,8},{10,11... | collective-permute-start | bytes 208904 | tf_op jit(solution)/shard_map/ppermute | solution.py:309
  91.3 1.9 %collective-permute-start.21 = (f32[128,128]{1,0:T(8,128)S(1)}, f32[128,128]{1,0:T(8,128)S(1)}, u32[]{:S(2)}, u32[]{:S(2)}) collective-permute-start(f32[128,128]{1,0:T(8,128)S(1)} %get-tuple-element.66.one_ref), channel_id=1, source_target_pairs={{0,2},{1,3},{2,0},{3,1},{4,6},{5,7},{6,4},{7,5},{8,10},{9,11},{10,... | collective-permute-start | bytes 196616 | tf_op jit(solution)/shard_map/ppermute | solution.py:309
  94.1 2.0 %collective-permute-start.19 = (f32[136,128]{1,0:T(8,128)S(1)}, f32[136,128]{1,0:T(8,128)S(1)}, u32[]{:S(2)}, u32[]{:S(2)}) collective-permute-start(f32[136,128]{1,0:T(8,128)S(1)} %add.24.one_ref), channel_id=1, source_target_pairs={{0,2},{1,3},{2,0},{3,1},{4,6},{5,7},{6,4},{7,5},{8,10},{9,11},{10,... | collective-permute-start | bytes 208904 | tf_op jit(solution)/shard_map/ppermute | solution.py:309
  98.5 2.0 %collective-permute-start.20 = (f32[136,128]{1,0:T(8,128)S(1)}, f32[136,128]{1,0:T(8,128)S(1)}, u32[]{:S(2)}, u32[]{:S(2)}) collective-permute-start(f32[136,128]{1,0:T(8,128)S(1)} %add.25.front), channel_id=1, source_target_pairs={{0,4},{1,5},{2,6},{3,7},{4,0},{5,1},{6,2},{7,3},{8,12},{9,13},{10,... | collective-permute-start | bytes 208904 | tf_op jit(solution)/shard_map/ppermute | solution.py:309
  100.6 2.0 %collective-permute-start.23 = (f32[128,128]{1,0:T(8,128)S(1)}, f32[128,128]{1,0:T(8,128)S(1)}, u32[]{:S(2)}, u32[]{:S(2)}) collective-permute-start(f32[128,128]{1,0:T(8,128)S(1)} %add.27.back), channel_id=1, source_target_pairs={{0,4},{1,5},{2,6},{3,7},{4,0},{5,1},{6,2},{7,3},{8,12},{9,13},{10,... | collective-permute-start | bytes 196616 | tf_op jit(solution)/shard_map/ppermute | solution.py:309
  102.6 3.3 %collective-permute-done.23.back_last = f32[128,128]{1,0:T(8,128)S(1)} collective-permute-done((f32[128,128]{1,0:T(8,128)S(1)}, f32[128,128]{1,0:T(8,128)S(1)}, u32[]{:S(2)}, u32[]{:S(2)}) %collective-permute-start.23) | collective-permute-done | bytes 65568 | tf_op jit(solution)/shard_map/ppermute | solution.py:309
  106.1 2.1 %own.5.partial_ref = f32[32,4096]{1,0:T(8,128)S(1)} custom-call(f32[32,1024]{1,0:T(8,128)S(1)} %get-tuple-element.70.clipped_ref, bf16[2048,4096]{1,0:T(8,128)(2,1)S(1)} %get-tuple-element.47.high_ref, f8e4m3fn[2048,4096]{1,0:T(32,128)(4,1)S(1)} %get-tuple-element.48.low_ref), custom_call_target="tpu_custom_call" | custom-call | tf_op jit(solution)/shard_map/own/pallas_call | solution.py:277
  109.0 5.8 %rest.5 = (f32[32,4096]{1,0:T(8,128)S(1)}, bf16[64,4096]{1,0:T(8,128)(2,1)S(1)}, f8e4m3fn[32,4096]{1,0:T(32,128)(4,1)S(1)}, f32[264,128]{1,0:T(8,128)S(1)}, f32[40,128]{1,0:T(8,128)S(1)}) custom-call(f32[32,1024]{1,0:T(8,128)S(1)} %collective-permute-done.25.clipped_ref, bf16[2048,4096]{1,0:T(8,128)(2,1)S(1)} %get-tuple-element.47.high_ref, ...), custom_call_target="tpu_custom_call" | custom-call | tf_op jit(solution)/shard_map/rest/pallas_call | solution.py:277
  115.3 3.7 %image.5.own_ref = f32[264,128]{1,0:T(8,128)S(1)} custom-call(bf16[64,4096]{1,0:T(8,128)(2,1)S(1)} %get-tuple-element.72.pair_ref, f8e4m3fn[32,4096]{1,0:T(32,128)(4,1)S(1)} %get-tuple-element.73.coarse_ref, f32[40,128]{1,0:T(8,128)S(1)} %get-tuple-element.74.notes_ref, bf16[2048,4096]{1,0:T(8,128)(2,1)S(1)} %get-tuple-element.47.high_ref, ...), custom_call_target="tpu_custom_call" | custom-call | tf_op jit(solution)/shard_map/image/pallas_call | solution.py:277
  123.5 2.0 %collective-permute-start.29 = (f32[136,128]{1,0:T(8,128)S(1)}, f32[136,128]{1,0:T(8,128)S(1)}, u32[]{:S(2)}, u32[]{:S(2)}) collective-permute-start(f32[136,128]{1,0:T(8,128)S(1)} %add.28.one_ref), channel_id=1, source_target_pairs={{0,2},{1,3},{2,0},{3,1},{4,6},{5,7},{6,4},{7,5},{8,10},{9,11},{10,... | collective-permute-start | bytes 208904 | tf_op jit(solution)/shard_map/ppermute | solution.py:309
  127.9 2.0 %collective-permute-start.30 = (f32[136,128]{1,0:T(8,128)S(1)}, f32[136,128]{1,0:T(8,128)S(1)}, u32[]{:S(2)}, u32[]{:S(2)}) collective-permute-start(f32[136,128]{1,0:T(8,128)S(1)} %add.29.front), channel_id=1, source_target_pairs={{0,4},{1,5},{2,6},{3,7},{4,0},{5,1},{6,2},{7,3},{8,12},{9,13},{10,... | collective-permute-start | bytes 208904 | tf_op jit(solution)/shard_map/ppermute | solution.py:309
  131.5 3.7 %collective-permute-done.33.back_last = f32[128,128]{1,0:T(8,128)S(1)} collective-permute-done((f32[128,128]{1,0:T(8,128)S(1)}, f32[128,128]{1,0:T(8,128)S(1)}, u32[]{:S(2)}, u32[]{:S(2)}) %collective-permute-start.33) | collective-permute-done | bytes 65568 | tf_op jit(solution)/shard_map/ppermute | solution.py:309
  (86 shorter events, 28.0 us)
Async XLA Ops:
  0.6 2.3 %collective-permute-start = (s32[1024,128]{1,0:T(8,128)}, s32[1024,128]{1,0:T(8,128)S(1)}, u32[]{:S(2)}, u32[]{:S(2)}) collective-permute-start(s32[1024,128]{1,0:T(8,128)} %own_ref.1), channel_id=1, source_target_pairs={{0,8},{8,0},{1,9},{9,1},{2,10},{10,2},{3,11},{11,3},{4,12},{12,4},... | collective-permute-start | bytes 1572872 | tf_op jit(solution)/shard_map/ppermute | solution.py:299
  31.0 5.3 %collective-permute-start.2 = (f32[128,128]{1,0:T(8,128)S(1)}, f32[128,128]{1,0:T(8,128)S(1)}, u32[]{:S(2)}, u32[]{:S(2)}) collective-permute-start(f32[128,128]{1,0:T(8,128)S(1)} %get-tuple-element.44.one_ref), channel_id=1, source_target_pairs={{0,1},{1,0},{2,3},{3,2},{4,5},{5,4},{6,7},{7,6},{8,9},{9,8},{10,11... | collective-permute-start | bytes 196616 | tf_op jit(solution)/shard_map/ppermute | solution.py:309
  33.7 4.5 %collective-permute-start.5 = (f32[128,128]{1,0:T(8,128)S(1)}, f32[128,128]{1,0:T(8,128)S(1)}, u32[]{:S(2)}, u32[]{:S(2)}) collective-permute-start(f32[128,128]{1,0:T(8,128)S(1)} %get-tuple-element.45.one_ref), channel_id=1, source_target_pairs={{0,2},{1,3},{2,0},{3,1},{4,6},{5,7},{6,4},{7,5},{8,10},{9,11},{10,... | collective-permute-start | bytes 196616 | tf_op jit(solution)/shard_map/ppermute | solution.py:309
  36.4 4.3 %collective-permute-start.3 = (f32[128,128]{1,0:T(8,128)S(1)}, f32[128,128]{1,0:T(8,128)S(1)}, u32[]{:S(2)}, u32[]{:S(2)}) collective-permute-start(f32[128,128]{1,0:T(8,128)S(1)} %add.16.one_ref), channel_id=1, source_target_pairs={{0,2},{1,3},{2,0},{3,1},{4,6},{5,7},{6,4},{7,5},{8,10},{9,11},{10,... | collective-permute-start | bytes 196616 | tf_op jit(solution)/shard_map/ppermute | solution.py:309
  38.2 5.3 %collective-permute-start.6 = (f32[128,128]{1,0:T(8,128)S(1)}, f32[128,128]{1,0:T(8,128)S(1)}, u32[]{:S(2)}, u32[]{:S(2)}) collective-permute-start(f32[128,128]{1,0:T(8,128)S(1)} %add.18.one_ref), channel_id=1, source_target_pairs={{0,1},{1,0},{2,3},{3,2},{4,5},{5,4},{6,7},{7,6},{8,9},{9,8},{10,11... | collective-permute-start | bytes 196616 | tf_op jit(solution)/shard_map/ppermute | solution.py:309
  40.7 7.3 %collective-permute-start.4 = (f32[128,128]{1,0:T(8,128)S(1)}, f32[128,128]{1,0:T(8,128)S(1)}, u32[]{:S(2)}, u32[]{:S(2)}) collective-permute-start(f32[128,128]{1,0:T(8,128)S(1)} %add.17.front), channel_id=1, source_target_pairs={{0,4},{1,5},{2,6},{3,7},{4,0},{5,1},{6,2},{7,3},{8,12},{9,13},{10,... | collective-permute-start | bytes 196616 | tf_op jit(solution)/shard_map/ppermute | solution.py:309
  43.6 5.2 %collective-permute-start.7 = (f32[128,128]{1,0:T(8,128)S(1)}, f32[128,128]{1,0:T(8,128)S(1)}, u32[]{:S(2)}, u32[]{:S(2)}) collective-permute-start(f32[128,128]{1,0:T(8,128)S(1)} %add.19.back), channel_id=1, source_target_pairs={{0,4},{1,5},{2,6},{3,7},{4,0},{5,1},{6,2},{7,3},{8,12},{9,13},{10,... | collective-permute-start | bytes 196616 | tf_op jit(solution)/shard_map/ppermute | solution.py:309
  56.9 4.2 %collective-permute-start.9 = (f32[264,128]{1,0:T(8,128)S(1)}, f32[264,128]{1,0:T(8,128)S(1)}, u32[]{:S(2)}, u32[]{:S(2)}) collective-permute-start(f32[264,128]{1,0:T(8,128)S(1)} %get-tuple-element.54), channel_id=1, source_target_pairs={{0,8},{8,0},{1,9},{9,1},{2,10},{10,2},{3,11},{11,3},{4,12},{12,4},... | collective-permute-start | bytes 405512 | tf_op jit(solution)/shard_map/ppermute | solution.py:299
  61.1 4.4 %collective-permute-start.10 = (f32[136,128]{1,0:T(8,128)S(1)}, f32[136,128]{1,0:T(8,128)S(1)}, u32[]{:S(2)}, u32[]{:S(2)}) collective-permute-start(f32[136,128]{1,0:T(8,128)S(1)} %get-tuple-element.55.one_ref), channel_id=1, source_target_pairs={{0,1},{1,0},{2,3},{3,2},{4,5},{5,4},{6,7},{7,6},{8,9},{9,8},{10,11... | collective-permute-start | bytes 208904 | tf_op jit(solution)/shard_map/ppermute | solution.py:309
  62.7 4.4 %collective-permute-start.13 = (f32[128,128]{1,0:T(8,128)S(1)}, f32[128,128]{1,0:T(8,128)S(1)}, u32[]{:S(2)}, u32[]{:S(2)}) collective-permute-start(f32[128,128]{1,0:T(8,128)S(1)} %get-tuple-element.56.one_ref), channel_id=1, source_target_pairs={{0,2},{1,3},{2,0},{3,1},{4,6},{5,7},{6,4},{7,5},{8,10},{9,11},{10,... | collective-permute-start | bytes 196616 | tf_op jit(solution)/shard_map/ppermute | solution.py:309
  65.5 4.4 %collective-permute-start.11 = (f32[136,128]{1,0:T(8,128)S(1)}, f32[136,128]{1,0:T(8,128)S(1)}, u32[]{:S(2)}, u32[]{:S(2)}) collective-permute-start(f32[136,128]{1,0:T(8,128)S(1)} %add.20.one_ref), channel_id=1, source_target_pairs={{0,2},{1,3},{2,0},{3,1},{4,6},{5,7},{6,4},{7,5},{8,10},{9,11},{10,... | collective-permute-start | bytes 208904 | tf_op jit(solution)/shard_map/ppermute | solution.py:309
  67.2 4.5 %collective-permute-start.14 = (f32[128,128]{1,0:T(8,128)S(1)}, f32[128,128]{1,0:T(8,128)S(1)}, u32[]{:S(2)}, u32[]{:S(2)}) collective-permute-start(f32[128,128]{1,0:T(8,128)S(1)} %add.22.one_ref), channel_id=1, source_target_pairs={{0,1},{1,0},{2,3},{3,2},{4,5},{5,4},{6,7},{7,6},{8,9},{9,8},{10,11... | collective-permute-start | bytes 196616 | tf_op jit(solution)/shard_map/ppermute | solution.py:309
  69.9 7.1 %collective-permute-start.12 = (f32[136,128]{1,0:T(8,128)S(1)}, f32[136,128]{1,0:T(8,128)S(1)}, u32[]{:S(2)}, u32[]{:S(2)}) collective-permute-start(f32[136,128]{1,0:T(8,128)S(1)} %add.21.front), channel_id=1, source_target_pairs={{0,4},{1,5},{2,6},{3,7},{4,0},{5,1},{6,2},{7,3},{8,12},{9,13},{10,... | collective-permute-start | bytes 208904 | tf_op jit(solution)/shard_map/ppermute | solution.py:309
  71.7 5.4 %collective-permute-start.15 = (f32[128,128]{1,0:T(8,128)S(1)}, f32[128,128]{1,0:T(8,128)S(1)}, u32[]{:S(2)}, u32[]{:S(2)}) collective-permute-start(f32[128,128]{1,0:T(8,128)S(1)} %add.23.back), channel_id=1, source_target_pairs={{0,4},{1,5},{2,6},{3,7},{4,0},{5,1},{6,2},{7,3},{8,12},{9,13},{10,... | collective-permute-start | bytes 196616 | tf_op jit(solution)/shard_map/ppermute | solution.py:309
  77.2 2.2 %collective-permute-start.16 = (f32[32,1024]{1,0:T(8,128)S(1)}, f32[32,1024]{1,0:T(8,128)S(1)}, u32[]{:S(2)}, u32[]{:S(2)}) collective-permute-start(f32[32,1024]{1,0:T(8,128)S(1)} %get-tuple-element.59.clipped_ref), channel_id=1, source_target_pairs={{0,8},{8,0},{1,9},{9,1},{2,10},{10,2},{3,11},{11,3},{4,12},{12,4},... | collective-permute-start | bytes 393224 | tf_op jit(solution)/shard_map/ppermute | solution.py:299
  85.5 4.2 %collective-permute-start.17 = (f32[264,128]{1,0:T(8,128)S(1)}, f32[264,128]{1,0:T(8,128)S(1)}, u32[]{:S(2)}, u32[]{:S(2)}) collective-permute-start(f32[264,128]{1,0:T(8,128)S(1)} %get-tuple-element.64), channel_id=1, source_target_pairs={{0,8},{8,0},{1,9},{9,1},{2,10},{10,2},{3,11},{11,3},{4,12},{12,4},... | collective-permute-start | bytes 405512 | tf_op jit(solution)/shard_map/ppermute | solution.py:299
  89.7 4.4 %collective-permute-start.18 = (f32[136,128]{1,0:T(8,128)S(1)}, f32[136,128]{1,0:T(8,128)S(1)}, u32[]{:S(2)}, u32[]{:S(2)}) collective-permute-start(f32[136,128]{1,0:T(8,128)S(1)} %get-tuple-element.65.one_ref), channel_id=1, source_target_pairs={{0,1},{1,0},{2,3},{3,2},{4,5},{5,4},{6,7},{7,6},{8,9},{9,8},{10,11... | collective-permute-start | bytes 208904 | tf_op jit(solution)/shard_map/ppermute | solution.py:309
  91.3 4.8 %collective-permute-start.21 = (f32[128,128]{1,0:T(8,128)S(1)}, f32[128,128]{1,0:T(8,128)S(1)}, u32[]{:S(2)}, u32[]{:S(2)}) collective-permute-start(f32[128,128]{1,0:T(8,128)S(1)} %get-tuple-element.66.one_ref), channel_id=1, source_target_pairs={{0,2},{1,3},{2,0},{3,1},{4,6},{5,7},{6,4},{7,5},{8,10},{9,11},{10,... | collective-permute-start | bytes 196616 | tf_op jit(solution)/shard_map/ppermute | solution.py:309
  94.1 4.4 %collective-permute-start.19 = (f32[136,128]{1,0:T(8,128)S(1)}, f32[136,128]{1,0:T(8,128)S(1)}, u32[]{:S(2)}, u32[]{:S(2)}) collective-permute-start(f32[136,128]{1,0:T(8,128)S(1)} %add.24.one_ref), channel_id=1, source_target_pairs={{0,2},{1,3},{2,0},{3,1},{4,6},{5,7},{6,4},{7,5},{8,10},{9,11},{10,... | collective-permute-start | bytes 208904 | tf_op jit(solution)/shard_map/ppermute | solution.py:309
  96.1 4.4 %collective-permute-start.22 = (f32[128,128]{1,0:T(8,128)S(1)}, f32[128,128]{1,0:T(8,128)S(1)}, u32[]{:S(2)}, u32[]{:S(2)}) collective-permute-start(f32[128,128]{1,0:T(8,128)S(1)} %add.26.one_ref), channel_id=1, source_target_pairs={{0,1},{1,0},{2,3},{3,2},{4,5},{5,4},{6,7},{7,6},{8,9},{9,8},{10,11... | collective-permute-start | bytes 196616 | tf_op jit(solution)/shard_map/ppermute | solution.py:309
  98.5 7.4 %collective-permute-start.20 = (f32[136,128]{1,0:T(8,128)S(1)}, f32[136,128]{1,0:T(8,128)S(1)}, u32[]{:S(2)}, u32[]{:S(2)}) collective-permute-start(f32[136,128]{1,0:T(8,128)S(1)} %add.25.front), channel_id=1, source_target_pairs={{0,4},{1,5},{2,6},{3,7},{4,0},{5,1},{6,2},{7,3},{8,12},{9,13},{10,... | collective-permute-start | bytes 208904 | tf_op jit(solution)/shard_map/ppermute | solution.py:309
  100.6 5.3 %collective-permute-start.23 = (f32[128,128]{1,0:T(8,128)S(1)}, f32[128,128]{1,0:T(8,128)S(1)}, u32[]{:S(2)}, u32[]{:S(2)}) collective-permute-start(f32[128,128]{1,0:T(8,128)S(1)} %add.27.back), channel_id=1, source_target_pairs={{0,4},{1,5},{2,6},{3,7},{4,0},{5,1},{6,2},{7,3},{8,12},{9,13},{10,... | collective-permute-start | bytes 196616 | tf_op jit(solution)/shard_map/ppermute | solution.py:309
  106.1 2.9 %collective-permute-start.25 = (f32[32,1024]{1,0:T(8,128)S(1)}, f32[32,1024]{1,0:T(8,128)S(1)}, u32[]{:S(2)}, u32[]{:S(2)}) collective-permute-start(f32[32,1024]{1,0:T(8,128)S(1)} %get-tuple-element.70.clipped_ref), channel_id=1, source_target_pairs={{0,8},{8,0},{1,9},{9,1},{2,10},{10,2},{3,11},{11,3},{4,12},{12,4},... | collective-permute-start | bytes 393224 | tf_op jit(solution)/shard_map/ppermute | solution.py:299
  108.4 27.7 %collective-permute-start.24 = (f32[32,4096]{1,0:T(8,128)S(1)}, f32[32,4096]{1,0:T(8,128)S(1)}, u32[]{:S(2)}, u32[]{:S(2)}) collective-permute-start(f32[32,4096]{1,0:T(8,128)S(1)} %sum.1.taken_ref), channel_id=1, source_target_pairs={{0,8},{8,0},{1,9},{9,1},{2,10},{10,2},{3,11},{11,3},{4,12},{12,4},... | collective-permute-start | bytes 1572872 | tf_op jit(solution)/shard_map/ppermute | solution.py:299
  114.8 21.3 %collective-permute-start.26 = (f32[32,4096]{1,0:T(8,128)S(1)}, f32[32,4096]{1,0:T(8,128)S(1)}, u32[]{:S(2)}, u32[]{:S(2)}) collective-permute-start(f32[32,4096]{1,0:T(8,128)S(1)} %get-tuple-element.71.grad_ref), channel_id=1, source_target_pairs={{0,8},{8,0},{1,9},{9,1},{2,10},{10,2},{3,11},{11,3},{4,12},{12,4},... | collective-permute-start | bytes 1572872 | tf_op jit(solution)/shard_map/ppermute | solution.py:299
  114.9 4.2 %collective-permute-start.27 = (f32[264,128]{1,0:T(8,128)S(1)}, f32[264,128]{1,0:T(8,128)S(1)}, u32[]{:S(2)}, u32[]{:S(2)}) collective-permute-start(f32[264,128]{1,0:T(8,128)S(1)} %get-tuple-element.75), channel_id=1, source_target_pairs={{0,8},{8,0},{1,9},{9,1},{2,10},{10,2},{3,11},{11,3},{4,12},{12,4},... | collective-permute-start | bytes 405512 | tf_op jit(solution)/shard_map/ppermute | solution.py:299
  119.1 4.4 %collective-permute-start.28 = (f32[136,128]{1,0:T(8,128)S(1)}, f32[136,128]{1,0:T(8,128)S(1)}, u32[]{:S(2)}, u32[]{:S(2)}) collective-permute-start(f32[136,128]{1,0:T(8,128)S(1)} %get-tuple-element.76.one_ref), channel_id=1, source_target_pairs={{0,1},{1,0},{2,3},{3,2},{4,5},{5,4},{6,7},{7,6},{8,9},{9,8},{10,11... | collective-permute-start | bytes 208904 | tf_op jit(solution)/shard_map/ppermute | solution.py:309
  120.6 4.8 %collective-permute-start.31 = (f32[128,128]{1,0:T(8,128)S(1)}, f32[128,128]{1,0:T(8,128)S(1)}, u32[]{:S(2)}, u32[]{:S(2)}) collective-permute-start(f32[128,128]{1,0:T(8,128)S(1)} %get-tuple-element.77.one_ref), channel_id=1, source_target_pairs={{0,2},{1,3},{2,0},{3,1},{4,6},{5,7},{6,4},{7,5},{8,10},{9,11},{10,... | collective-permute-start | bytes 196616 | tf_op jit(solution)/shard_map/ppermute | solution.py:309
  123.5 4.4 %collective-permute-start.29 = (f32[136,128]{1,0:T(8,128)S(1)}, f32[136,128]{1,0:T(8,128)S(1)}, u32[]{:S(2)}, u32[]{:S(2)}) collective-permute-start(f32[136,128]{1,0:T(8,128)S(1)} %add.28.one_ref), channel_id=1, source_target_pairs={{0,2},{1,3},{2,0},{3,1},{4,6},{5,7},{6,4},{7,5},{8,10},{9,11},{10,... | collective-permute-start | bytes 208904 | tf_op jit(solution)/shard_map/ppermute | solution.py:309
  125.5 4.4 %collective-permute-start.32 = (f32[128,128]{1,0:T(8,128)S(1)}, f32[128,128]{1,0:T(8,128)S(1)}, u32[]{:S(2)}, u32[]{:S(2)}) collective-permute-start(f32[128,128]{1,0:T(8,128)S(1)} %add.30.one_ref), channel_id=1, source_target_pairs={{0,1},{1,0},{2,3},{3,2},{4,5},{5,4},{6,7},{7,6},{8,9},{9,8},{10,11... | collective-permute-start | bytes 196616 | tf_op jit(solution)/shard_map/ppermute | solution.py:309
  127.9 7.3 %collective-permute-start.30 = (f32[136,128]{1,0:T(8,128)S(1)}, f32[136,128]{1,0:T(8,128)S(1)}, u32[]{:S(2)}, u32[]{:S(2)}) collective-permute-start(f32[136,128]{1,0:T(8,128)S(1)} %add.29.front), channel_id=1, source_target_pairs={{0,4},{1,5},{2,6},{3,7},{4,0},{5,1},{6,2},{7,3},{8,12},{9,13},{10,... | collective-permute-start | bytes 208904 | tf_op jit(solution)/shard_map/ppermute | solution.py:309
  129.9 5.3 %collective-permute-start.33 = (f32[128,128]{1,0:T(8,128)S(1)}, f32[128,128]{1,0:T(8,128)S(1)}, u32[]{:S(2)}, u32[]{:S(2)}) collective-permute-start(f32[128,128]{1,0:T(8,128)S(1)} %add.31.back), channel_id=1, source_target_pairs={{0,4},{1,5},{2,6},{3,7},{4,0},{5,1},{6,2},{7,3},{8,12},{9,13},{10,... | collective-permute-start | bytes 196616 | tf_op jit(solution)/shard_map/ppermute | solution.py:309
  (8 other events, 61.2 us)
